TPU v7x, 32 devices: a whole 2x2x4 slice. The times are simulated.
32 devices in a mesh: runs: 2 (over y), sec: 4 (over z), ops: 2 (over x), sub: 2 (over core).
Axes of the slice: x: 2, y: 2, z: 4, core: 2. Of those that a mesh axis runs over, the one named last changes fastest.
Arguments:
- psi: bfloat16 [4, 4, 4, 128, 512], P('runs', 'sec', None, None, 'sub'), parts along dimension 0, may hold values from -6 to 6
- left_op: bfloat16 [16, 4, 128, 128], P(('runs', 'ops'), 'sec'), parts along dimension 0, may hold values from -0.5 to 0.5
- right_op: bfloat16 [16, 4, 512, 512], P(('runs', 'ops'), 'sec', None, 'sub'), parts along dimension 0, may hold values from -0.09375 to 0.09375
- sector_rows: int32 [8], P('runs'), parts along dimension 0, may hold values from 32 to 128, as said below
- block_live: int32 [8, 4], P('runs'), parts along dimension 0, may hold values 0 or 1
Outputs:
- sigma: bfloat16 [4, 4, 4, 128, 512], P('runs', None, 'sec', 'ops', 'sub'), parts along dimension 0
There are 2 independent parts, one for each index of `runs`. A program takes and returns all parts, laid end to end along the dimension named above; each array names one. Nothing has to cross between parts.
Inputs may be any that keep to these rules, and one draw needn't show every extreme that they name: `sector_rows`: the number of row slots that each left sector uses; some sector uses all 128.
All inputs are finite; a program needn't handle non-finite values.
Results may differ from a plain program's by a relative error of at most 0.0059.
Values may be sent and summed in bfloat16 or wider, within the bound.
No kernel may reach another device: no remote copies, remote signals or barrier semaphores. Data moves between devices by JAX's collectives and lax.ppermute only.
A program may use at most 64 MiB of HBM per device.

v0:
```python
import jax
import jax.numpy as jnp
from jax import lax
from jax.sharding import PartitionSpec as P


def local(psi, left_op, right_op, sector_rows, block_live):
    vectors, sec_dev, sectors, block_rows, half_cols = psi.shape
    terms = left_op.shape[0]
    own_rows = block_rows // lax.axis_size("ops")
    sec_start = lax.axis_index("sec") * sec_dev
    row_ids = lax.broadcasted_iota(jnp.int32, (sectors, block_rows), 1)
    row_keep = row_ids < sector_rows[:, None]
    live_right = lax.dynamic_slice_in_dim(block_live, sec_start, sec_dev, 1)
    keep_right = row_keep[:, None, :, None] & (live_right[:, :, None, None] > 0)
    empty = jnp.zeros((vectors, sectors, sec_dev, block_rows, half_cols), jnp.float32)
    moved = lax.all_to_all(psi, "sec", split_axis=2, concat_axis=1, tiled=True)
    moved = jnp.where(keep_right[None], moved, jnp.zeros_like(moved))
    lefts = lax.all_gather(left_op, "sec", axis=1, tiled=True)
    piece = lax.all_gather(moved, "sub", axis=4, tiled=True)

    def one_term(index, acc):
        left_part = jnp.einsum(
            "aij,vacjk->vacik", lefts[index], piece, preferred_element_type=jnp.float32
        ).astype(jnp.bfloat16)
        right_rows = right_op[index]
        return acc + jnp.einsum(
            "vacik,ckl->vacil", left_part, right_rows, preferred_element_type=jnp.float32
        )

    partial_value = lax.fori_loop(0, terms, one_term, empty)
    summed = lax.psum(partial_value.astype(jnp.bfloat16), "ops").astype(jnp.float32)
    own = lax.dynamic_slice_in_dim(summed, lax.axis_index("ops") * own_rows, own_rows, 3)
    keep_own = lax.dynamic_slice_in_dim(keep_right, lax.axis_index("ops") * own_rows, own_rows, 2)
    total = jnp.where(keep_own[None], own, jnp.zeros_like(own))
    return total.astype(jnp.bfloat16)


def solution(mesh):
    return jax.shard_map(
        local,
        mesh=mesh,
        in_specs=(
            P("runs", "sec", None, None, "sub"),
            P(("runs", "ops"), "sec", None, None),
            P(("runs", "ops"), "sec", None, "sub"),
            P("runs"),
            P("runs", None),
        ),
        out_specs=P("runs", None, "sec", "ops", "sub"),
        check_vma=False,
    )
```

profile of v0, /device:TPU:0, one launch (start us, length us, event | category | flops | bytes accessed | tf_op | source)
XLA Modules:
  0.0 96.8 jit_solution(12545271838397749866)
XLA Ops:
  6.5 0.0 copy-start.1
  6.5 0.0 copy-start.2
  6.5 1.9 %copy.11 = bf16[2,1,4,128,256]{4,3,0,1,2:T(8,128)(2,1)} copy(bf16[2,1,4,128,256]{4,3,2,1,0:T(8,128)(2,1)} %param.7) | data formatting | bytes 1048576 | tf_op args[0]
  8.4 6.3 %all-to-all-start = ((bf16[2,1,4,128,256]{4,3,0,1,2:T(8,128)(2,1)}), bf16[2,1,4,128,256]{4,3,0,1,2:T(8,128)(2,1)S(1)}, u32[]{:S(2)}, u32[]{:S(2)}) async-start(bf16[2,1,4,128,256]{4,3,0,1,2:T(8,128)(2,1)} %copy.11), calls=%async_computation | async-start | bytes 1048576 | tf_op jit(solution)/shard_map/all_to_all | solution.py:17
  14.8 0.0 copy-start
  14.8 0.0 all-gather.2.cloned.1.call-start
  14.8 0.0 copy-done.1
  14.8 0.2 fusion.11
  15.0 0.0 copy-done.2
  15.0 0.1 fusion.12
  15.0 14.2 %all-to-all-done = bf16[2,1,4,128,256]{4,3,0,1,2:T(8,128)(2,1)S(1)} async-done(((bf16[2,1,4,128,256]{4,3,0,1,2:T(8,128)(2,1)}), bf16[2,1,4,128,256]{4,3,0,1,2:T(8,128)(2,1)S(1)}, u32[]{:S(2)}, u32[]{:S(2)}) %all-to-all-start) | async-done | bytes 524320 | tf_op jit(solution)/shard_map/all_to_all | solution.py:17
  29.2 0.9 bitcast_select_fusion
  30.2 0.0 all-gather.2.cloned.1.call-update
  30.2 0.0 all-reduce.2.cloned.1.call-start
  30.3 0.0 copy-done
  30.3 15.9 %all_gather.6 = bf16[4,4,128,128]{3,2,1,0:T(8,128)(2,1)S(1)} all-gather(bf16[4,1,128,128]{3,2,1,0:T(8,128)(2,1)S(1)} %copy-done), channel_id=1, replica_groups=mesh['runs'=2,'sec'=4,'ops'=2,'sub'=2] {'sec'}, dimensions={1}, use_global_device_ids=true | all-gather | bytes 655360 | tf_op jit(solution)/shard_map/all_gather | solution.py:19
  46.2 0.0 all-gather.2.cloned.1.call-done
  46.2 13.3 %while.14 = (s32[]{:T(128)}, f32[2,4,1,128,256]{3,4,1,0,2:T(8,128)S(1)}, bf16[4,1,512,256]{3,2,1,0:T(8,128)(2,1)}, bf16[4,4,128,128]{3,2,1,0:T(8,128)(2,1)S(1)},...) while((s32[]{:T(128)}, f32[2,4,1,128,256]{3,4,1,0,2:T(8,128)S(1)}, ...), condition=%wide.region_1.2_spmd.clone, body=%wide.region_0.1_spmd.clone.sunk | while | flops 403701760 | bytes 5636699 | solution.py:31
  46.2 1.6 %fusion.23 = bf16[2,4,128,512]{3,2,0,1:T(8,128)(2,1)S(1)} fusion(bf16[2,4,1,128,512]{4,3,0,1,2:T(8,128)(2,1)} %get-tuple-element.187, bf16[4,4,128,128]{3,2,1,0:T(8,128)(2,1)S(1)} %get-tuple-element.186, s32[]{:T(128)} %get-tuple-element.176), kind=kOutput, calls=%fused_computation.1.clone.1 | convolution fusion | flops 134742016 | bytes 2228228 | tf_op jit(solution)/shard_map/while/body/eval_jaxpr/aij,vacjk->vacik/dot_general | solution.py:23
  47.9 1.6 %fusion.24 = f32[2,4,1,128,256]{3,4,1,0,2:T(8,128)S(1)} fusion(bf16[2,4,128,512]{3,2,0,1:T(8,128)(2,1)S(1)} %fusion.23, f32[2,4,1,128,256]{3,4,1,0,2:T(8,128)S(1)} %get-tuple-element.177, pred[]{:T(512)S(6)} %compare.3, bf16[4,1,512,256]{3,2,1,0:T(8,128)(2,1)} %get-tuple-element.185, s32[]{:T(128)} %get-tuple-element.176), kind=kOutput, calls=%fused_computation.3.clone.1 | convolution fusion | flops 268959744 | bytes 3408385 | tf_op jit(solution)/shard_map/while/body/eval_jaxpr/vacik,ckl->vacil/dot_general | solution.py:27
  49.5 1.6 %fusion.23 = bf16[2,4,128,512]{3,2,0,1:T(8,128)(2,1)S(1)} fusion(bf16[2,4,1,128,512]{4,3,0,1,2:T(8,128)(2,1)} %get-tuple-element.187, bf16[4,4,128,128]{3,2,1,0:T(8,128)(2,1)S(1)} %get-tuple-element.186, s32[]{:T(128)} %get-tuple-element.176), kind=kOutput, calls=%fused_computation.1.clone.1 | convolution fusion | flops 134742016 | bytes 2228228 | tf_op jit(solution)/shard_map/while/body/eval_jaxpr/aij,vacjk->vacik/dot_general | solution.py:23
  51.2 1.6 %fusion.24 = f32[2,4,1,128,256]{3,4,1,0,2:T(8,128)S(1)} fusion(bf16[2,4,128,512]{3,2,0,1:T(8,128)(2,1)S(1)} %fusion.23, f32[2,4,1,128,256]{3,4,1,0,2:T(8,128)S(1)} %get-tuple-element.177, pred[]{:T(512)S(6)} %compare.3, bf16[4,1,512,256]{3,2,1,0:T(8,128)(2,1)} %get-tuple-element.185, s32[]{:T(128)} %get-tuple-element.176), kind=kOutput, calls=%fused_computation.3.clone.1 | convolution fusion | flops 268959744 | bytes 3408385 | tf_op jit(solution)/shard_map/while/body/eval_jaxpr/vacik,ckl->vacil/dot_general | solution.py:27
  52.8 1.6 %fusion.23 = bf16[2,4,128,512]{3,2,0,1:T(8,128)(2,1)S(1)} fusion(bf16[2,4,1,128,512]{4,3,0,1,2:T(8,128)(2,1)} %get-tuple-element.187, bf16[4,4,128,128]{3,2,1,0:T(8,128)(2,1)S(1)} %get-tuple-element.186, s32[]{:T(128)} %get-tuple-element.176), kind=kOutput, calls=%fused_computation.1.clone.1 | convolution fusion | flops 134742016 | bytes 2228228 | tf_op jit(solution)/shard_map/while/body/eval_jaxpr/aij,vacjk->vacik/dot_general | solution.py:23
  54.5 1.6 %fusion.24 = f32[2,4,1,128,256]{3,4,1,0,2:T(8,128)S(1)} fusion(bf16[2,4,128,512]{3,2,0,1:T(8,128)(2,1)S(1)} %fusion.23, f32[2,4,1,128,256]{3,4,1,0,2:T(8,128)S(1)} %get-tuple-element.177, pred[]{:T(512)S(6)} %compare.3, bf16[4,1,512,256]{3,2,1,0:T(8,128)(2,1)} %get-tuple-element.185, s32[]{:T(128)} %get-tuple-element.176), kind=kOutput, calls=%fused_computation.3.clone.1 | convolution fusion | flops 268959744 | bytes 3408385 | tf_op jit(solution)/shard_map/while/body/eval_jaxpr/vacik,ckl->vacil/dot_general | solution.py:27
  56.2 1.6 %fusion.23 = bf16[2,4,128,512]{3,2,0,1:T(8,128)(2,1)S(1)} fusion(bf16[2,4,1,128,512]{4,3,0,1,2:T(8,128)(2,1)} %get-tuple-element.187, bf16[4,4,128,128]{3,2,1,0:T(8,128)(2,1)S(1)} %get-tuple-element.186, s32[]{:T(128)} %get-tuple-element.176), kind=kOutput, calls=%fused_computation.1.clone.1 | convolution fusion | flops 134742016 | bytes 2228228 | tf_op jit(solution)/shard_map/while/body/eval_jaxpr/aij,vacjk->vacik/dot_general | solution.py:23
  57.8 1.6 %fusion.24 = f32[2,4,1,128,256]{3,4,1,0,2:T(8,128)S(1)} fusion(bf16[2,4,128,512]{3,2,0,1:T(8,128)(2,1)S(1)} %fusion.23, f32[2,4,1,128,256]{3,4,1,0,2:T(8,128)S(1)} %get-tuple-element.177, pred[]{:T(512)S(6)} %compare.3, bf16[4,1,512,256]{3,2,1,0:T(8,128)(2,1)} %get-tuple-element.185, s32[]{:T(128)} %get-tuple-element.176), kind=kOutput, calls=%fused_computation.3.clone.1 | convolution fusion | flops 268959744 | bytes 3408385 | tf_op jit(solution)/shard_map/while/body/eval_jaxpr/vacik,ckl->vacil/dot_general | solution.py:27
  59.5 1.0 %copy.13 = bf16[2,4,1,128,256]{4,3,2,1,0:T(8,128)(2,1)} copy(f32[2,4,1,128,256]{3,4,1,0,2:T(8,128)S(1)} %get-tuple-element.99) | data formatting | bytes 1572864 | tf_op jit(solution)/shard_map/while | solution.py:31
  60.5 0.0 all-reduce.2.cloned.1.call-update
  60.5 0.1 fusion.10
  60.6 0.1 dynamic-slice_bitcast_fusion
  60.6 27.6 %all-reduce.2.cloned.1.call-done = bf16[2,4,1,128,256]{4,3,2,1,0:T(8,128)(2,1)} async-done(((bf16[2,4,1,128,256]{4,3,2,1,0:T(8,128)(2,1)}), bf16[2,4,1,128,256]{4,3,2,1,0:T(8,128)(2,1)}) %all-reduce.2.cloned.1.call-update) | async-done | bytes 524304 | tf_op jit(solution)/shard_map/psum | solution.py:32
  88.2 1.8 %select_convert_fusion = bf16[2,4,1,64,256]{4,3,2,1,0:T(8,128)(2,1)} fusion(bf16[2,4,1,128,256]{4,3,2,1,0:T(8,128)(2,1)} %all-reduce.2.cloned.1.call-done, s32[]{:T(128)S(6)} %select_n.30, pred[4,64]{1,0:T(4,128)(4,1)S(1)} %dynamic-slice_bitcast_fusion), kind=kLoop, calls=%fused_computation.13 | loop fusion | flops 393216 | bytes 524548 | tf_op jit(solution)/shard_map/convert_element_type | solution.py:36
  (1 shorter events, 0.0 us)
Async XLA Ops:
  6.5 8.2 %copy-start.1 = (s32[4,4]{1,0:T(4,128)S(1)}, s32[4,4]{1,0:T(4,128)}, u32[]{:S(2)}) copy-start(s32[4,4]{1,0:T(4,128)} %param.11) | copy-start | bytes 196
  6.5 8.4 %copy-start.2 = (s32[4]{0:T(128)S(1)}, s32[4]{0:T(128)}, u32[]{:S(2)}) copy-start(s32[4]{0:T(128)} %param.10) | copy-start | bytes 52
  8.4 20.8 %all-to-all-start = ((bf16[2,1,4,128,256]{4,3,0,1,2:T(8,128)(2,1)}), bf16[2,1,4,128,256]{4,3,0,1,2:T(8,128)(2,1)S(1)}, u32[]{:S(2)}, u32[]{:S(2)}) async-start(bf16[2,1,4,128,256]{4,3,0,1,2:T(8,128)(2,1)} %copy.11), calls=%async_computation | async-start | bytes 1048576 | tf_op jit(solution)/shard_map/all_to_all | solution.py:17
  14.8 15.5 %copy-start = (bf16[4,1,128,128]{3,2,1,0:T(8,128)(2,1)S(1)}, bf16[4,1,128,128]{3,2,1,0:T(8,128)(2,1)}, u32[]{:S(2)}) copy-start(bf16[4,1,128,128]{3,2,1,0:T(8,128)(2,1)} %param.8) | copy-start | bytes 393220
  14.8 31.4 %all-gather.2.cloned.1.call-start = ((), (), s32[]{:S(2)}) async-start(), calls=%async_computation.1 | async-start | bytes 1572864 | tf_op jit(solution)/shard_map/all_gather | solution.py:20
  30.2 58.0 %all-reduce.2.cloned.1.call-start = ((), (), s32[]{:S(2)}) async-start(), calls=%async_computation.2 | async-start | bytes 1048576 | tf_op jit(solution)/shard_map/psum | solution.py:32
Sparse Core Ops, SparseCore 0:
  30.3 8.0 all-gather.1
  60.6 27.5 all-reduce.1
where the time goes:
time: 97.4 us; the launch traced here: 96.8 us
  waiting for transfers between devices  41.8 us (43%)
  blocking collectives  15.9 us (16%)
  between operations  13.4 us (14%)
  matrix products  13.1 us (13%)
  starting transfers between devices  6.36 us (7%)
  other arithmetic  3.05 us (3%)
  local copies, waits for them, and re-layouts  2.98 us (3%)
    psum x1, waiting for transfers between devices, local(): lax.psum(partial_value.astype(jnp.bfloat16), 'ops').astype(jnp.float32)  27.6 us
    all_gather x1, blocking collectives, local(): lefts = lax.all_gather(left_op, 'sec', axis=1, tiled=True)  15.9 us
    all_to_all x1, waiting for transfers between devices, local(): moved = lax.all_to_all(psi, 'sec', split_axis=2, concat_axis=1, tiled=True)  14.2 us
    dot_general x4, matrix products, one_term(): jnp.einsum('aij,vacjk->vacik', lefts[index], piece, preferred_element_typ...  6.58 us
    dot_general x4, matrix products, one_term(): jnp.einsum('vacik,ckl->vacil', left_part, right_rows, preferred_element_t...  6.56 us
    all_to_all x1, starting transfers between devices, local(): moved = lax.all_to_all(psi, 'sec', split_axis=2, concat_axis=1, tiled=True)  6.32 us
  transfers between devices with their start and end apart: 3, of which 2 were waited for; matrix products, arithmetic and copies ran while one was open for 0% of the time, Pallas kernels for 0%

commit v1 on v0

--- a/solution.py
+++ b/solution.py
@@ -1,10 +1,156 @@
+import functools
+import itertools
+
 import jax
 import jax.numpy as jnp
 from jax import lax
+from jax.experimental import pallas as pl
+from jax.experimental.pallas import tpu as pltpu
 from jax.sharding import PartitionSpec as P
 
+VMEM = pl.BlockSpec(memory_space=pltpu.VMEM)
+SMEM = pl.BlockSpec(memory_space=pltpu.SMEM)
 
-def local(psi, left_op, right_op, sector_rows, block_live):
+
+def joint_pairs(sizes, target):
+    places = list(itertools.product(*[range(size) for size in sizes]))
+    index = {place: number for number, place in enumerate(places)}
+    return [(index[place], index[target(*place)]) for place in places]
+
+
+def sector_product(mine, other, right, left, rows, half):
+    vectors, block_rows, half_cols = mine.shape
+    terms = right.shape[0]
+    x_mine = mine.reshape(vectors * block_rows, half_cols)
+    x_other = other.reshape(vectors * block_rows, half_cols)
+    mid = []
+    for term in range(terms):
+        near_rows = right[term, pl.ds(pl.multiple_of(half * half_cols, half_cols), half_cols), :]
+        far_rows = right[term, pl.ds(pl.multiple_of((1 - half) * half_cols, half_cols), half_cols), :]
+        value = jnp.dot(x_mine, near_rows, preferred_element_type=jnp.float32)
+        value = value + jnp.dot(x_other, far_rows, preferred_element_type=jnp.float32)
+        mid.append(value.astype(jnp.bfloat16).reshape(vectors, block_rows, -1))
+    keep = lax.broadcasted_iota(jnp.int32, (block_rows, block_rows), 1) < rows
+    wide = jnp.concatenate(
+        [jnp.where(keep, left[term], jnp.zeros_like(left[term])) for term in range(terms)], axis=1
+    )
+    out = []
+    for vector in range(vectors):
+        tall = jnp.concatenate([mid[term][vector] for term in range(terms)], axis=0)
+        out.append(jnp.dot(wide, tall, preferred_element_type=jnp.float32))
+    return out
+
+
+def store_halves(values, own, send_ref, keep_ref, slot):
+    own_rows = keep_ref.shape[2]
+    for vector, value in enumerate(values):
+        low, high = value[:own_rows], value[own_rows:]
+        keep_ref[slot, vector] = jnp.where(own == 0, low, high)
+        send_ref[slot, vector] = jnp.where(own == 0, high, low).astype(send_ref.dtype)
+
+
+def blocks_kernel(sources, *refs):
+    count = len(sources)
+    rows_ref, right = refs[0], refs[1]
+    blocks = refs[2:2 + 3 * count]
+    send_ref, keep_ref = refs[2 + 3 * count:]
+    me, own, half = lax.axis_index("sec"), lax.axis_index("ops"), lax.axis_index("sub")
+    for number, (source, slot) in enumerate(sources):
+        mine, other, left = blocks[3 * number:3 * number + 3]
+        rows = rows_ref[me ^ source(own)]
+        values = sector_product(mine[...], other[...], right, left, rows, half)
+        store_halves(values, own, send_ref, keep_ref, slot(own))
+
+
+def blocks_call(sources, rows, right, blocks):
+    vectors, block_rows, half_cols = blocks[0].shape
+    shape = (len(sources), vectors, block_rows // 2, right.shape[2])
+    return pl.pallas_call(
+        functools.partial(blocks_kernel, sources),
+        out_shape=(
+            jax.ShapeDtypeStruct(shape, jnp.bfloat16),
+            jax.ShapeDtypeStruct(shape, jnp.float32),
+        ),
+        in_specs=[SMEM] + [VMEM] * (1 + len(blocks)),
+        out_specs=(VMEM, VMEM),
+        compiler_params=pltpu.CompilerParams(vmem_limit_bytes=24 << 20),
+    )(rows, right, *blocks)
+
+
+def final_kernel(sources, rows_ref, live_ref, *refs):
+    out_ref = refs[-1]
+    me, own = lax.axis_index("sec"), lax.axis_index("ops")
+    vectors, own_rows, columns = out_ref.shape[0], out_ref.shape[3], out_ref.shape[4]
+    row_ids = own * own_rows + lax.broadcasted_iota(jnp.int32, (own_rows, columns), 0)
+    for number in range(len(sources)):
+        keep_ref, got_ref = refs[2 * number], refs[2 * number + 1]
+        for slot, offset in enumerate(sources[number]):
+            sector = me ^ offset
+            rows = jnp.where(live_ref[sector, me] > 0, rows_ref[sector], 0)
+            for vector in range(vectors):
+                total = keep_ref[slot, vector] + got_ref[slot, vector].astype(jnp.float32)
+                total = jnp.where(row_ids < rows, total, jnp.zeros_like(total))
+                out_ref[vector, sector, 0] = total.astype(out_ref.dtype)
+
+
+def final_call(sources, rows, live, parts, shape):
+    return pl.pallas_call(
+        functools.partial(final_kernel, sources),
+        out_shape=jax.ShapeDtypeStruct(shape, jnp.bfloat16),
+        in_specs=[SMEM, SMEM] + [VMEM] * len(parts),
+        out_specs=VMEM,
+        compiler_params=pltpu.CompilerParams(vmem_limit_bytes=24 << 20),
+    )(rows, live, *parts)
+
+
+def local_small(psi, left_op, right_op, sector_rows, block_live):
+    vectors, sec_dev, sectors, block_rows, half_cols = psi.shape
+    me, own = lax.axis_index("sec"), lax.axis_index("ops")
+    swap = [(0, 1), (1, 0)]
+    near_pairs = [(z, z ^ 1) for z in range(4)]
+    far_pairs = joint_pairs((4, 2), lambda z, o: (z ^ (2 + o), o))
+
+    def pick(sector):
+        return lax.dynamic_index_in_dim(psi[:, 0], sector, 1, keepdims=False)
+
+    far = pick(me ^ (2 + own))
+    near = pick(me ^ 1)
+    mine = pick(me)
+    left = left_op[:, 0]
+    right = right_op[:, 0]
+
+    far_in = lax.ppermute(far, ("sec", "ops"), far_pairs)
+    left_far = lax.ppermute(left, ("sec", "sub"), far_pairs)
+    near_in = lax.ppermute(near, "sec", near_pairs)
+    left_near = lax.ppermute(left, "sec", near_pairs)
+    mine_other = lax.ppermute(mine, "sub", swap)
+    near_other = lax.ppermute(near_in, "sub", swap)
+    left_far_other = lax.ppermute(left_far, "sub", swap)
+    far_swapped = lax.ppermute(far_in, "ops", swap)
+    far_other = lax.ppermute(far_in, "sub", swap)
+    swapped_other = lax.ppermute(far_swapped, "sub", swap)
+
+    sub = lax.axis_index("sub")
+    first_left = jnp.where(sub == own, left_far, left_far_other)
+    second_left = jnp.where(sub == own, left_far_other, left_far)
+
+    send_a, keep_a = blocks_call(
+        ((lambda o: 0, lambda o: 0), (lambda o: 1, lambda o: 1)),
+        sector_rows, right, (mine, mine_other, left, near_in, near_other, left_near),
+    )
+    got_a = lax.ppermute(send_a, "ops", swap)
+    send_b, keep_b = blocks_call(
+        ((lambda o: 2 + o, lambda o: o), (lambda o: 3 - o, lambda o: 1 - o)),
+        sector_rows, right, (far_in, far_other, first_left, far_swapped, swapped_other, second_left),
+    )
+    got_b = lax.ppermute(send_b, "ops", swap)
+    shape = (vectors, sectors, sec_dev, block_rows // 2, right.shape[2])
+    return final_call(
+        ((0, 1), (2, 3)), sector_rows, block_live, (keep_a, got_a, keep_b, got_b), shape
+    )
+
+
+def local_any(psi, left_op, right_op, sector_rows, block_live):
     vectors, sec_dev, sectors, block_rows, half_cols = psi.shape
     terms = left_op.shape[0]
     own_rows = block_rows // lax.axis_size("ops")
@@ -20,12 +166,11 @@
     piece = lax.all_gather(moved, "sub", axis=4, tiled=True)
 
     def one_term(index, acc):
-        left_part = jnp.einsum(
-            "aij,vacjk->vacik", lefts[index], piece, preferred_element_type=jnp.float32
+        mid = jnp.einsum(
+            "vacjk,ckl->vacjl", piece, right_op[index], preferred_element_type=jnp.float32
         ).astype(jnp.bfloat16)
-        right_rows = right_op[index]
         return acc + jnp.einsum(
-            "vacik,ckl->vacil", left_part, right_rows, preferred_element_type=jnp.float32
+            "aij,vacjl->vacil", lefts[index], mid, preferred_element_type=jnp.float32
         )
 
     partial_value = lax.fori_loop(0, terms, one_term, empty)
@@ -37,8 +182,10 @@
 
 
 def solution(mesh):
+    sizes = dict(mesh.shape)
+    small = sizes["sec"] == 4 and sizes["ops"] == 2 and sizes["sub"] == 2
     return jax.shard_map(
-        local,
+        local_small if small else local_any,
         mesh=mesh,
         in_specs=(
             P("runs", "sec", None, None, "sub"),

time: 97.4 us -> 33.7 us (0.35)
  waiting for transfers between devices: 41.8 us -> 17.3 us
  blocking collectives: 15.9 us -> 0 us
  between operations: 13.4 us -> 0.06 us
  matrix products: 13.1 us -> 0 us
  Pallas kernels: 0 us -> 4.56 us
  other arithmetic: 3.05 us -> 0.02 us
  starting transfers between devices: 6.36 us -> 9.1 us
    psum x1 -> x0, waiting for transfers between devices: 27.6 us -> none  [local(): lax.psum(partial_value.astype(jnp.bfloat16), 'ops').astype(jnp.float32)]
    ppermute x0 -> x12, waiting for transfers between devices: none -> 17.3 us  [the longest x1 7.89 us: local_small(): far_in = lax.ppermute(far, ('sec', 'ops'), far_pairs)]
    all_gather x1 -> x0, blocking collectives: 15.9 us -> none  [local(): lefts = lax.all_gather(left_op, 'sec', axis=1, tiled=True)]
    all_to_all x1 -> x0, waiting for transfers between devices: 14.2 us -> none  [local(): moved = lax.all_to_all(psi, 'sec', split_axis=2, concat_axis=1, tiled=True)]
    dot_general x8 -> x0, matrix products: 13.1 us -> none  [the longest x4 6.58 us: one_term(): jnp.einsum('aij,vacjk->vacik', lefts[index], piece, preferred_element_typ...]
    ppermute x0 -> x12, starting transfers between devices: none -> 9.1 us  [the longest x1 3.09 us: local_small(): near_in = lax.ppermute(near, 'sec', near_pairs)]
    all_to_all x1 -> x0, starting transfers between devices: 6.32 us -> none  [local(): moved = lax.all_to_all(psi, 'sec', split_axis=2, concat_axis=1, tiled=True)]
    pallas_call x0 -> x3, Pallas kernels: none -> 4.56 us  [the longest x2 3.21 us: blocks_call(): pl.pallas_call(functools.partial(blocks_kernel, sources), out_shape=(jax....]
  transfers between devices with their start and end apart: 3 -> 12, of which waited for: 2 -> 6; matrix products, arithmetic and copies ran while one was open for 0% -> 0% of each run, Pallas kernels for 0% -> 10%
where the time goes in v1:
time: 33.7 us; the launch traced here: 33.5 us
  waiting for transfers between devices  17.3 us (51%)
  starting transfers between devices  9.1 us (27%)
  Pallas kernels  4.56 us (14%)
  local copies, waits for them, and re-layouts  2.47 us (7%)
    ppermute x1, waiting for transfers between devices, local_small(): far_in = lax.ppermute(far, ('sec', 'ops'), far_pairs)  7.89 us
    ppermute x1, waiting for transfers between devices, local_small(): got_b = lax.ppermute(send_b, 'ops', swap)  4.14 us
    pallas_call x2, Pallas kernels, blocks_call(): pl.pallas_call(functools.partial(blocks_kernel, sources), out_shape=(jax....  3.21 us
    ppermute x1, starting transfers between devices, local_small(): near_in = lax.ppermute(near, 'sec', near_pairs)  3.09 us
    ppermute x1, starting transfers between devices, local_small(): far_in = lax.ppermute(far, ('sec', 'ops'), far_pairs)  2.59 us
    ppermute x1, waiting for transfers between devices, local_small(): near_in = lax.ppermute(near, 'sec', near_pairs)  1.92 us
    ppermute x1, starting transfers between devices, local_small(): got_a = lax.ppermute(send_a, 'ops', swap)  1.45 us
    ppermute x1, waiting for transfers between devices, local_small(): left_far = lax.ppermute(left, ('sec', 'sub'), far_pairs)  1.4 us
  transfers between devices with their start and end apart: 12, of which 6 were waited for; matrix products, arithmetic and copies ran while one was open for 0% of the time, Pallas kernels for 10%

profile of v1, /device:TPU:0, one launch (start us, length us, event | category | flops | bytes accessed | tf_op | source)
XLA Modules:
  0.0 33.5 jit_solution(1856928616284310560)
XLA Ops:
  0.0 0.0 copy-start.1
  0.0 1.1 %dynamic-slice_bitcast_fusion = (bf16[2,128,256]{2,1,0:T(8,128)(2,1)S(1)}, bf16[2,128,256]{2,1,0:T(8,128)(2,1)S(1)}, bf16[2,128,256]{2,1,0:T(8,128)(2,1)S(1)}) fusion(bf16[2,1,4,128,256]{4,3,2,1,0:T(8,128)(2,1)} %param.5, s32[]{:T(128)S(6)} %select_n.24, s32[]{:T(128)S(6)} %select_n.22, s32[]{:T(128)S(6)} %select_n.23), kind=kLoop, calls=%fused_computation | loop fusion | bytes 786444 | tf_op jit(solution)/shard_map/jit(dynamic_index_in_dim)/squeeze | solution.py:114
  1.1 3.1 %collective-permute-start.1 = (bf16[2,128,256]{2,1,0:T(8,128)(2,1)S(1)}, bf16[2,128,256]{2,1,0:T(8,128)(2,1)S(1)}, u32[]{:S(2)}, u32[]{:S(2)}) collective-permute-start(bf16[2,128,256]{2,1,0:T(8,128)(2,1)S(1)} %get-tuple-element.15), channel_id=1, source_target_pairs={{0,4},{4,0},{8,12},{12,8},{1,5},{5,1},{9,13},{13,9},{2,6},{6,2},{1... | collective-permute-start | bytes 393224 | tf_op jit(solution)/shard_map/ppermute | solution.py:124
  4.2 2.6 %collective-permute-start.5 = (bf16[2,128,256]{2,1,0:T(8,128)(2,1)S(1)}, bf16[2,128,256]{2,1,0:T(8,128)(2,1)S(1)}, u32[]{:S(2)}, u32[]{:S(2)}) collective-permute-start(bf16[2,128,256]{2,1,0:T(8,128)(2,1)S(1)} %get-tuple-element.13), channel_id=1, source_target_pairs={{0,8},{2,14},{4,12},{6,10},{8,0},{10,6},{12,4},{14,2},{1,9},{3,15}... | collective-permute-start | bytes 393224 | tf_op jit(solution)/shard_map/ppermute | solution.py:122
  6.8 0.0 copy-done.1
  6.8 0.3 %collective-permute-start.7 = (bf16[4,128,128]{2,1,0:T(8,128)(2,1)S(1)}, bf16[4,128,128]{2,1,0:T(8,128)(2,1)S(1)}, u32[]{:S(2)}, u32[]{:S(2)}) collective-permute-start(bf16[4,128,128]{2,1,0:T(8,128)(2,1)S(1)} %bitcast.10), channel_id=1, source_target_pairs={{0,8},{1,13},{4,12},{5,9},{8,0},{9,5},{12,4},{13,1},{2,10},{3,15},... | collective-permute-start | bytes 393224 | tf_op jit(solution)/shard_map/ppermute | solution.py:123
  7.1 0.0 collective-permute-start
  7.1 0.2 collective-permute-start.3
  7.3 1.9 %collective-permute-done.1.refs_5_ = bf16[2,128,256]{2,1,0:T(8,128)(2,1)S(1)} collective-permute-done((bf16[2,128,256]{2,1,0:T(8,128)(2,1)S(1)}, bf16[2,128,256]{2,1,0:T(8,128)(2,1)S(1)}, u32[]{:S(2)}, u32[]{:S(2)}) %collective-permute-start.1) | collective-permute-done | bytes 131104 | tf_op jit(solution)/shard_map/ppermute | solution.py:124
  9.2 0.0 collective-permute-start.2
  9.2 7.9 %collective-permute-done.5.refs_2_ = bf16[2,128,256]{2,1,0:T(8,128)(2,1)S(1)} collective-permute-done((bf16[2,128,256]{2,1,0:T(8,128)(2,1)S(1)}, bf16[2,128,256]{2,1,0:T(8,128)(2,1)S(1)}, u32[]{:S(2)}, u32[]{:S(2)}) %collective-permute-start.5) | collective-permute-done | bytes 131104 | tf_op jit(solution)/shard_map/ppermute | solution.py:122
  17.1 0.0 collective-permute-start.9
  17.1 1.4 %collective-permute-done.7 = bf16[4,128,128]{2,1,0:T(8,128)(2,1)S(1)} collective-permute-done((bf16[4,128,128]{2,1,0:T(8,128)(2,1)S(1)}, bf16[4,128,128]{2,1,0:T(8,128)(2,1)S(1)}, u32[]{:S(2)}, u32[]{:S(2)}) %collective-permute-start.7) | collective-permute-done | bytes 131104 | tf_op jit(solution)/shard_map/ppermute | solution.py:123
  18.5 0.0 collective-permute-start.8
  18.5 0.0 copy-start.2
  18.5 0.0 collective-permute-done.refs_3_
  18.5 0.5 %collective-permute-start.6 = (bf16[2,128,256]{2,1,0:T(8,128)(2,1)S(1)}, bf16[2,128,256]{2,1,0:T(8,128)(2,1)S(1)}, u32[]{:S(2)}, u32[]{:S(2)}) collective-permute-start(bf16[2,128,256]{2,1,0:T(8,128)(2,1)S(1)} %collective-permute-done.5.refs_2_), channel_id=1, source_target_pairs={{0,1},{1,0},{2,3},{3,2},{4,5},{5,4},{6,7},{7,6},{8,9},{9,8},{10,11... | collective-permute-start | bytes 393224 | tf_op jit(solution)/shard_map/ppermute | solution.py:130
  19.0 0.0 collective-permute-done.3.refs_7_
  19.0 0.0 collective-permute-done.2.refs_6_
  19.0 0.1 copy-done.2
  19.2 0.0 copy-start
  19.2 1.2 %copy-done = bf16[4,1,512,256]{3,2,1,0:T(8,128)(2,1)S(1)} copy-done((bf16[4,1,512,256]{3,2,1,0:T(8,128)(2,1)S(1)}, bf16[4,1,512,256]{3,2,1,0:T(8,128)(2,1)}, u32[]{:S(2)}) %copy-start) | copy-done | bytes 1048600
  20.4 1.6 %shard_map.55 = (bf16[2,2,64,256]{3,2,1,0:T(8,128)(2,1)S(1)}, f32[2,2,64,256]{3,2,1,0:T(8,128)S(1)}) custom-call(s32[4]{0:T(128)S(1)} %copy-done.2, bf16[4,512,256]{2,1,0:T(8,128)(2,1)S(1)} %bitcast.8, bf16[2,128,256]{2,1,0:T(8,128)(2,1)S(1)} %get-tuple-element.14.refs_2_, bf16[2,128,256]{2,1,0:T(8,128)(2,1)S(1)} %collective-permute-done.refs_3_, ...), custom_call_target="tpu_custom_call" | custom-call | tf_op jit(solution)/shard_map/pallas_call | solution.py:68
  22.0 1.5 %collective-permute-start.4 = (bf16[2,2,64,256]{3,2,1,0:T(8,128)(2,1)S(1)}, bf16[2,2,64,256]{3,2,1,0:T(8,128)(2,1)S(1)}, u32[]{:S(2)}, u32[]{:S(2)}) collective-permute-start(bf16[2,2,64,256]{3,2,1,0:T(8,128)(2,1)S(1)} %get-tuple-element.10), channel_id=1, source_target_pairs={{0,2},{2,0},{1,3},{3,1},{4,6},{6,4},{5,7},{7,5},{8,10},{10,8},{9,1... | collective-permute-start | bytes 393224 | tf_op jit(solution)/shard_map/ppermute | solution.py:141
  23.5 0.0 collective-permute-done.9.refs_5_
  23.5 0.2 collective-permute-start.10
  23.7 0.0 collective-permute-done.8
  23.7 0.0 collective-permute-done.6.refs_3_
  23.8 1.1 %collective-permute-done.10.refs_6_ = bf16[2,128,256]{2,1,0:T(8,128)(2,1)S(1)} collective-permute-done((bf16[2,128,256]{2,1,0:T(8,128)(2,1)S(1)}, bf16[2,128,256]{2,1,0:T(8,128)(2,1)S(1)}, u32[]{:S(2)}, u32[]{:S(2)}) %collective-permute-start.10) | collective-permute-done | bytes 131104 | tf_op jit(solution)/shard_map/ppermute | solution.py:131
  24.8 1.6 %shard_map.56 = (bf16[2,2,64,256]{3,2,1,0:T(8,128)(2,1)S(1)}, f32[2,2,64,256]{3,2,1,0:T(8,128)S(1)}) custom-call(s32[4]{0:T(128)S(1)} %copy-done.2, bf16[4,512,256]{2,1,0:T(8,128)(2,1)S(1)} %bitcast.9, bf16[2,128,256]{2,1,0:T(8,128)(2,1)S(1)} %collective-permute-done.5.refs_2_, bf16[2,128,256]{2,1,0:T(8,128)(2,1)S(1)} %collective-permute-done.6.refs_3_, ...), custom_call_target="tpu_custom_call" | custom-call | tf_op jit(solution)/shard_map/pallas_call | solution.py:68
  26.4 0.0 copy-start.3
  26.4 0.7 %collective-permute-start.11 = (bf16[2,2,64,256]{3,2,1,0:T(8,128)(2,1)S(1)}, bf16[2,2,64,256]{3,2,1,0:T(8,128)(2,1)S(1)}, u32[]{:S(2)}, u32[]{:S(2)}) collective-permute-start(bf16[2,2,64,256]{3,2,1,0:T(8,128)(2,1)S(1)} %get-tuple-element.12), channel_id=1, source_target_pairs={{0,2},{2,0},{1,3},{3,1},{4,6},{6,4},{5,7},{7,5},{8,10},{10,8},{9,1... | collective-permute-start | bytes 393224 | tf_op jit(solution)/shard_map/ppermute | solution.py:146
  27.1 0.8 %collective-permute-done.4.refs_1_ = bf16[2,2,64,256]{3,2,1,0:T(8,128)(2,1)S(1)} collective-permute-done((bf16[2,2,64,256]{3,2,1,0:T(8,128)(2,1)S(1)}, bf16[2,2,64,256]{3,2,1,0:T(8,128)(2,1)S(1)}, u32[]{:S(2)}, u32[]{:S(2)}) %collective-permute-start.4) | collective-permute-done | bytes 131104 | tf_op jit(solution)/shard_map/ppermute | solution.py:141
  28.0 4.1 %collective-permute-done.11.refs_3_ = bf16[2,2,64,256]{3,2,1,0:T(8,128)(2,1)S(1)} collective-permute-done((bf16[2,2,64,256]{3,2,1,0:T(8,128)(2,1)S(1)}, bf16[2,2,64,256]{3,2,1,0:T(8,128)(2,1)S(1)}, u32[]{:S(2)}, u32[]{:S(2)}) %collective-permute-start.11) | collective-permute-done | bytes 131104 | tf_op jit(solution)/shard_map/ppermute | solution.py:146
  32.1 0.0 copy-done.3
  32.1 1.4 %shard_map.57 = bf16[2,4,1,64,256]{4,3,2,1,0:T(8,128)(2,1)} custom-call(s32[4]{0:T(128)S(1)} %copy-done.2, s32[4,4]{1,0:T(4,128)S(1)} %copy-done.3, f32[2,2,64,256]{3,2,1,0:T(8,128)S(1)} %get-tuple-element.9.refs_0_, bf16[2,2,64,256]{3,2,1,0:T(8,128)(2,1)S(1)} %collective-permute-done.4.refs_1_, f32[2,2,64,256]{3,2,1,0:T(8,128)S(1)} %get-tuple-element.11.refs_2_, ...), custom_call_target="tpu_custom_call" | custom-call | tf_op jit(solution)/shard_map/pallas_call | solution.py:97
  (1 shorter events, 0.0 us)
Async XLA Ops:
  0.0 6.8 %copy-start.1 = (bf16[4,1,128,128]{3,2,1,0:T(8,128)(2,1)S(1)}, bf16[4,1,128,128]{3,2,1,0:T(8,128)(2,1)}, u32[]{:S(2)}) copy-start(bf16[4,1,128,128]{3,2,1,0:T(8,128)(2,1)} %param.6) | copy-start | bytes 393220
  1.1 8.1 %collective-permute-start.1 = (bf16[2,128,256]{2,1,0:T(8,128)(2,1)S(1)}, bf16[2,128,256]{2,1,0:T(8,128)(2,1)S(1)}, u32[]{:S(2)}, u32[]{:S(2)}) collective-permute-start(bf16[2,128,256]{2,1,0:T(8,128)(2,1)S(1)} %get-tuple-element.15), channel_id=1, source_target_pairs={{0,4},{4,0},{8,12},{12,8},{1,5},{5,1},{9,13},{13,9},{2,6},{6,2},{1... | collective-permute-start | bytes 393224 | tf_op jit(solution)/shard_map/ppermute | solution.py:124
  4.2 12.9 %collective-permute-start.5 = (bf16[2,128,256]{2,1,0:T(8,128)(2,1)S(1)}, bf16[2,128,256]{2,1,0:T(8,128)(2,1)S(1)}, u32[]{:S(2)}, u32[]{:S(2)}) collective-permute-start(bf16[2,128,256]{2,1,0:T(8,128)(2,1)S(1)} %get-tuple-element.13), channel_id=1, source_target_pairs={{0,8},{2,14},{4,12},{6,10},{8,0},{10,6},{12,4},{14,2},{1,9},{3,15}... | collective-permute-start | bytes 393224 | tf_op jit(solution)/shard_map/ppermute | solution.py:122
  6.8 11.7 %collective-permute-start.7 = (bf16[4,128,128]{2,1,0:T(8,128)(2,1)S(1)}, bf16[4,128,128]{2,1,0:T(8,128)(2,1)S(1)}, u32[]{:S(2)}, u32[]{:S(2)}) collective-permute-start(bf16[4,128,128]{2,1,0:T(8,128)(2,1)S(1)} %bitcast.10), channel_id=1, source_target_pairs={{0,8},{1,13},{4,12},{5,9},{8,0},{9,5},{12,4},{13,1},{2,10},{3,15},... | collective-permute-start | bytes 393224 | tf_op jit(solution)/shard_map/ppermute | solution.py:123
  7.1 11.4 %collective-permute-start = (bf16[2,128,256]{2,1,0:T(8,128)(2,1)S(1)}, bf16[2,128,256]{2,1,0:T(8,128)(2,1)S(1)}, u32[]{:S(2)}, u32[]{:S(2)}) collective-permute-start(bf16[2,128,256]{2,1,0:T(8,128)(2,1)S(1)} %get-tuple-element.14.refs_2_), channel_id=1, source_target_pairs={{0,1},{1,0},{2,3},{3,2},{4,5},{5,4},{6,7},{7,6},{8,9},{9,8},{10,11... | collective-permute-start | bytes 393224 | tf_op jit(solution)/shard_map/ppermute | solution.py:126
  7.1 11.9 %collective-permute-start.3 = (bf16[4,128,128]{2,1,0:T(8,128)(2,1)S(1)}, bf16[4,128,128]{2,1,0:T(8,128)(2,1)S(1)}, u32[]{:S(2)}, u32[]{:S(2)}) collective-permute-start(bf16[4,128,128]{2,1,0:T(8,128)(2,1)S(1)} %bitcast.11), channel_id=1, source_target_pairs={{0,4},{4,0},{8,12},{12,8},{1,5},{5,1},{9,13},{13,9},{2,6},{6,2},{1... | collective-permute-start | bytes 393224 | tf_op jit(solution)/shard_map/ppermute | solution.py:125
  9.2 9.8 %collective-permute-start.2 = (bf16[2,128,256]{2,1,0:T(8,128)(2,1)S(1)}, bf16[2,128,256]{2,1,0:T(8,128)(2,1)S(1)}, u32[]{:S(2)}, u32[]{:S(2)}) collective-permute-start(bf16[2,128,256]{2,1,0:T(8,128)(2,1)S(1)} %collective-permute-done.1.refs_5_), channel_id=1, source_target_pairs={{0,1},{1,0},{2,3},{3,2},{4,5},{5,4},{6,7},{7,6},{8,9},{9,8},{10,11... | collective-permute-start | bytes 393224 | tf_op jit(solution)/shard_map/ppermute | solution.py:127
  17.1 6.4 %collective-permute-start.9 = (bf16[2,128,256]{2,1,0:T(8,128)(2,1)S(1)}, bf16[2,128,256]{2,1,0:T(8,128)(2,1)S(1)}, u32[]{:S(2)}, u32[]{:S(2)}) collective-permute-start(bf16[2,128,256]{2,1,0:T(8,128)(2,1)S(1)} %collective-permute-done.5.refs_2_), channel_id=1, source_target_pairs={{0,2},{2,0},{1,3},{3,1},{4,6},{6,4},{5,7},{7,5},{8,10},{10,8},{9,1... | collective-permute-start | bytes 393224 | tf_op jit(solution)/shard_map/ppermute | solution.py:129
  18.5 5.2 %collective-permute-start.8 = (bf16[4,128,128]{2,1,0:T(8,128)(2,1)S(1)}, bf16[4,128,128]{2,1,0:T(8,128)(2,1)S(1)}, u32[]{:S(2)}, u32[]{:S(2)}) collective-permute-start(bf16[4,128,128]{2,1,0:T(8,128)(2,1)S(1)} %collective-permute-done.7), channel_id=1, source_target_pairs={{0,1},{1,0},{2,3},{3,2},{4,5},{5,4},{6,7},{7,6},{8,9},{9,8},{10,11... | collective-permute-start | bytes 393224 | tf_op jit(solution)/shard_map/ppermute | solution.py:128
  18.5 0.7 %copy-start.2 = (s32[4]{0:T(128)S(1)}, s32[4]{0:T(128)}, u32[]{:S(2)}) copy-start(s32[4]{0:T(128)} %rows_ref.1) | copy-start | bytes 52
  18.5 5.2 %collective-permute-start.6 = (bf16[2,128,256]{2,1,0:T(8,128)(2,1)S(1)}, bf16[2,128,256]{2,1,0:T(8,128)(2,1)S(1)}, u32[]{:S(2)}, u32[]{:S(2)}) collective-permute-start(bf16[2,128,256]{2,1,0:T(8,128)(2,1)S(1)} %collective-permute-done.5.refs_2_), channel_id=1, source_target_pairs={{0,1},{1,0},{2,3},{3,2},{4,5},{5,4},{6,7},{7,6},{8,9},{9,8},{10,11... | collective-permute-start | bytes 393224 | tf_op jit(solution)/shard_map/ppermute | solution.py:130
  19.2 1.2 %copy-start = (bf16[4,1,512,256]{3,2,1,0:T(8,128)(2,1)S(1)}, bf16[4,1,512,256]{3,2,1,0:T(8,128)(2,1)}, u32[]{:S(2)}) copy-start(bf16[4,1,512,256]{3,2,1,0:T(8,128)(2,1)} %param.7) | copy-start | bytes 3145732
  22.0 6.0 %collective-permute-start.4 = (bf16[2,2,64,256]{3,2,1,0:T(8,128)(2,1)S(1)}, bf16[2,2,64,256]{3,2,1,0:T(8,128)(2,1)S(1)}, u32[]{:S(2)}, u32[]{:S(2)}) collective-permute-start(bf16[2,2,64,256]{3,2,1,0:T(8,128)(2,1)S(1)} %get-tuple-element.10), channel_id=1, source_target_pairs={{0,2},{2,0},{1,3},{3,1},{4,6},{6,4},{5,7},{7,5},{8,10},{10,8},{9,1... | collective-permute-start | bytes 393224 | tf_op jit(solution)/shard_map/ppermute | solution.py:141
  23.5 1.3 %collective-permute-start.10 = (bf16[2,128,256]{2,1,0:T(8,128)(2,1)S(1)}, bf16[2,128,256]{2,1,0:T(8,128)(2,1)S(1)}, u32[]{:S(2)}, u32[]{:S(2)}) collective-permute-start(bf16[2,128,256]{2,1,0:T(8,128)(2,1)S(1)} %collective-permute-done.9.refs_5_), channel_id=1, source_target_pairs={{0,1},{1,0},{2,3},{3,2},{4,5},{5,4},{6,7},{7,6},{8,9},{9,8},{10,11... | collective-permute-start | bytes 393224 | tf_op jit(solution)/shard_map/ppermute | solution.py:131
  26.4 5.7 %copy-start.3 = (s32[4,4]{1,0:T(4,128)S(1)}, s32[4,4]{1,0:T(4,128)}, u32[]{:S(2)}) copy-start(s32[4,4]{1,0:T(4,128)} %live_ref.1) | copy-start | bytes 196
  26.4 5.7 %collective-permute-start.11 = (bf16[2,2,64,256]{3,2,1,0:T(8,128)(2,1)S(1)}, bf16[2,2,64,256]{3,2,1,0:T(8,128)(2,1)S(1)}, u32[]{:S(2)}, u32[]{:S(2)}) collective-permute-start(bf16[2,2,64,256]{3,2,1,0:T(8,128)(2,1)S(1)} %get-tuple-element.12), channel_id=1, source_target_pairs={{0,2},{2,0},{1,3},{3,1},{4,6},{6,4},{5,7},{7,5},{8,10},{10,8},{9,1... | collective-permute-start | bytes 393224 | tf_op jit(solution)/shard_map/ppermute | solution.py:146

commit v2 on v0

--- a/solution.py
+++ b/solution.py
@@ -1,10 +1,210 @@
+import functools
+
 import jax
 import jax.numpy as jnp
 from jax import lax
+from jax.experimental import pallas as pl
+from jax.experimental.pallas import tpu as pltpu
 from jax.sharding import PartitionSpec as P
 
-
-def local(psi, left_op, right_op, sector_rows, block_live):
+VMEM = pl.BlockSpec(memory_space=pltpu.VMEM)
+SMEM = pl.BlockSpec(memory_space=pltpu.SMEM)
+
+
+def wide_left(low, high, rows):
+    wide = jnp.concatenate([low, high], axis=1)
+    block_rows = wide.shape[0]
+    column = lax.broadcasted_iota(jnp.int32, wide.shape, 1) % block_rows
+    return jnp.where(column < rows, wide, jnp.zeros_like(wide))
+
+
+def sector_product(mine, other, right, wide, half):
+    vectors, block_rows, half_cols = mine.shape
+    terms = right.shape[0]
+    x_mine = mine.reshape(vectors * block_rows, half_cols)
+    x_other = other.reshape(vectors * block_rows, half_cols)
+    mid = []
+    for term in range(terms):
+        near_rows = right[term, pl.ds(pl.multiple_of(half * half_cols, half_cols), half_cols), :]
+        far_rows = right[term, pl.ds(pl.multiple_of((1 - half) * half_cols, half_cols), half_cols), :]
+        value = jnp.dot(x_mine, near_rows, preferred_element_type=jnp.float32)
+        value = value + jnp.dot(x_other, far_rows, preferred_element_type=jnp.float32)
+        mid.append(value.astype(jnp.bfloat16).reshape(vectors, block_rows, -1))
+    out = []
+    for vector in range(vectors):
+        tall = jnp.concatenate([mid[term][vector] for term in range(terms)], axis=0)
+        out.append(jnp.dot(wide, tall, preferred_element_type=jnp.float32))
+    return out
+
+
+def store_halves(values, own, send_ref, keep_ref, slot):
+    own_rows = keep_ref.shape[2]
+    for vector, value in enumerate(values):
+        low, high = value[:own_rows], value[own_rows:]
+        keep_ref[slot, vector] = jnp.where(own == 0, low, high)
+        send_ref[slot, vector] = jnp.where(own == 0, high, low).astype(send_ref.dtype)
+
+
+def halves(mine, other, half):
+    return jnp.where(half == 0, mine, other), jnp.where(half == 0, other, mine)
+
+
+def by_vector(values, own):
+    return jnp.where(own == 0, values[0], values[1]), jnp.where(own == 0, values[1], values[0])
+
+
+def own_kernel(rows_ref, live_ref, right, left, mine, other, send_ref, keep_ref, used_ref, shown_ref):
+    me, own, half = lax.axis_index("sec"), lax.axis_index("ops"), lax.axis_index("sub")
+    sectors = rows_ref.shape[0]
+    for offset in range(sectors):
+        sector = me ^ offset
+        used = rows_ref[sector]
+        used_ref[offset] = jnp.full(used_ref.shape[1:], used, jnp.int32)
+        shown_ref[offset] = jnp.full(
+            shown_ref.shape[1:], jnp.where(live_ref[sector, me] > 0, used, 0), jnp.int32
+        )
+    low = jnp.concatenate([left[0], left[1]], axis=1)
+    high = jnp.concatenate([left[2], left[3]], axis=1)
+    values = sector_product(mine[...], other[...], right, wide_left(low, high, rows_ref[me]), half)
+    store_halves(values, own, send_ref, keep_ref, 0)
+
+
+def near_kernel(used_ref, right, near, other, send_ref, keep_ref):
+    own, half = lax.axis_index("ops"), lax.axis_index("sub")
+    wide = wide_left(*halves(near[2], other[2], half), used_ref[1, :1, :1])
+    values = sector_product(near[:2], other[:2], right, wide, half)
+    store_halves(values, own, send_ref, keep_ref, 0)
+
+
+def early_kernel(rows_ref, live_ref, right, left, mine, other, near, near_other,
+                 send_ref, keep_ref, used_ref, shown_ref):
+    own_kernel(rows_ref, live_ref, right, left, mine, other, send_ref.at[:1], keep_ref.at[:1], used_ref, shown_ref)
+    near_kernel(used_ref, right, near, near_other, send_ref.at[1:], keep_ref.at[1:])
+
+
+def far_kernel(plan, used_ref, right, *refs):
+    own, half = lax.axis_index("ops"), lax.axis_index("sub")
+    send_ref, keep_ref = refs[-2:]
+    for number, (offset, own_order) in enumerate(plan):
+        psi, other, left, left_other = refs[4 * number:4 * number + 4]
+        wide = wide_left(*halves(left[0], left_other[0], half), used_ref[offset, :1, :1])
+        values = sector_product(psi[:2], other[:2], right, wide, half)
+        if own_order:
+            values = by_vector(values, own)
+        store_halves(values, own, send_ref, keep_ref, number)
+
+
+PARAMS = pltpu.CompilerParams(vmem_limit_bytes=24 << 20)
+
+
+def cost(us):
+    return pl.CostEstimate(flops=int(us * 1.15e9), bytes_accessed=0, transcendentals=0)
+
+
+def blocks_call(kernel, count, right, *operands, scalars=(), extra=(), us=0):
+    columns = right.shape[2]
+    shape = (count, 2, right.shape[1] // 8, columns)
+    return pl.pallas_call(
+        kernel,
+        out_shape=(
+            jax.ShapeDtypeStruct(shape, jnp.bfloat16),
+            jax.ShapeDtypeStruct(shape, jnp.float32),
+            *extra,
+        ),
+        in_specs=[SMEM] * len(scalars) + [VMEM] * (len(operands)),
+        out_specs=(VMEM,) * (2 + len(extra)),
+        cost_estimate=cost(us),
+        compiler_params=PARAMS,
+    )(*scalars, *operands)
+
+
+def final_kernel(shown_ref, keep_m, got_m, keep_n, got_n, keep_b, got_b, keep_c, got_c, out_ref):
+    me, own = lax.axis_index("sec"), lax.axis_index("ops")
+    vectors, own_rows, columns = out_ref.shape[0], out_ref.shape[3], out_ref.shape[4]
+    row_ids = own * own_rows + lax.broadcasted_iota(jnp.int32, (own_rows, columns), 0)
+    pairs = (
+        (0, keep_m.at[0], got_m.at[0]), (1, keep_n.at[0], got_n.at[0]),
+        (3, keep_b.at[0], got_b.at[0]), (2, keep_c.at[0], got_c.at[0]),
+    )
+    for offset, keep_ref, got_ref in pairs:
+        keep = row_ids < shown_ref[offset, :1, :1]
+        for vector in range(vectors):
+            total = keep_ref[vector] + got_ref[vector].astype(jnp.float32)
+            total = jnp.where(keep, total, jnp.zeros_like(total))
+            out_ref[vector, me ^ offset, 0] = total.astype(out_ref.dtype)
+
+
+def final_call(shown, parts, shape):
+    return pl.pallas_call(
+        final_kernel,
+        out_shape=jax.ShapeDtypeStruct(shape, jnp.bfloat16),
+        in_specs=[VMEM] * (1 + len(parts)),
+        out_specs=VMEM,
+        cost_estimate=cost(0),
+        compiler_params=PARAMS,
+    )(shown, *parts)
+
+
+def local_small(psi, left_op, right_op, sector_rows, block_live):
+    vectors, sec_dev, sectors, block_rows, half_cols = psi.shape
+    me, own, half = lax.axis_index("sec"), lax.axis_index("ops"), lax.axis_index("sub")
+    right, left = right_op[:, 0], left_op[:, 0]
+    swap = [(0, 1), (1, 0)]
+
+    def exchange(value, offset):
+        return lax.ppermute(value, "sec", [(z, z ^ offset) for z in range(sectors)])
+
+    def in_pieces(value, axis_name, count):
+        if count == 1:
+            return lax.ppermute(value, axis_name, swap)
+        flat = value.reshape(-1, value.shape[-1])
+        parts = jnp.split(flat, count)
+        return jnp.concatenate([lax.ppermute(part, axis_name, swap) for part in parts]).reshape(value.shape)
+
+    def other_core(value, count=1):
+        return in_pieces(value, "sub", count)
+
+    def pick(vector, offset):
+        block = lax.dynamic_slice(
+            psi, (vector, 0, me ^ offset, 0, 0), (1, 1, 1, block_rows, half_cols)
+        )
+        return block.reshape(1, block_rows, half_cols)
+
+    pieces = [pick(0, 0), pick(1, 0), pick(0, 1), pick(1, 1), pick(0, 2), pick(1, 2), pick(own, 3)]
+    left_late, *pieces = lax.optimization_barrier((left, *pieces))
+    half_left = lax.dynamic_slice_in_dim(left_late, half * 2, 2, 0)
+    half_left = jnp.concatenate([half_left[0], half_left[1]], axis=1)[None]
+    mine = jnp.concatenate(pieces[:2])
+    near = jnp.concatenate([*pieces[2:4], half_left])
+    skip = jnp.concatenate([*pieces[4:6], half_left])
+    cross = jnp.concatenate([*pieces[6:], half_left])
+    rows_shape = jax.ShapeDtypeStruct((sectors, 8, 128), jnp.int32)
+    near_in = exchange(near, 1)
+    cross_in = exchange(cross, 3)
+    skip_in = exchange(skip, 2)
+    mine_other = other_core(mine, 2)
+    near_other = other_core(near_in, 3)
+    send_a, keep_a, used, shown = blocks_call(early_kernel, 2, right, right, left, mine, mine_other, near_in, near_other, scalars=(sector_rows, block_live), extra=(rows_shape, rows_shape), us=0)
+    got_a = in_pieces(send_a, "ops", 2)
+    cross_left = cross_in[1:]
+    cross_swapped = in_pieces(cross_in[:1], "ops", 1)
+    cross_swapped, got_a = lax.optimization_barrier((cross_swapped, got_a))
+    cross_psi = jnp.concatenate([cross_in[:1], cross_swapped])
+    cross_other = other_core(cross_psi, 2)
+    cross_left_other = other_core(cross_left, 1)
+    send_b, keep_b = blocks_call(functools.partial(far_kernel, ((3, True),)), 1, right, used, right, cross_psi, cross_other, cross_left, cross_left_other, us=0)
+    got_b = in_pieces(send_b, "ops", 1)
+    skip_in, send_b = lax.optimization_barrier((skip_in, send_b))
+    skip_other = other_core(skip_in, 3)
+    skip_left, skip_left_other = skip_in[2:], skip_other[2:]
+    send_c, keep_c = blocks_call(functools.partial(far_kernel, ((2, False),)), 1, right, used, right, skip_in, skip_other, skip_left, skip_left_other, us=0)
+    got_c = in_pieces(send_c, "ops", 1)
+    keep_m, keep_n, got_m, got_n = keep_a[:1], keep_a[1:], got_a[:1], got_a[1:]
+    shape = (vectors, sectors, sec_dev, block_rows // 2, half_cols)
+    return final_call(shown, (keep_m, got_m, keep_n, got_n, keep_b, got_b, keep_c, got_c), shape)
+
+
+def local_any(psi, left_op, right_op, sector_rows, block_live):
     vectors, sec_dev, sectors, block_rows, half_cols = psi.shape
     terms = left_op.shape[0]
     own_rows = block_rows // lax.axis_size("ops")
@@ -20,12 +220,11 @@
     piece = lax.all_gather(moved, "sub", axis=4, tiled=True)
 
     def one_term(index, acc):
-        left_part = jnp.einsum(
-            "aij,vacjk->vacik", lefts[index], piece, preferred_element_type=jnp.float32
+        mid = jnp.einsum(
+            "vacjk,ckl->vacjl", piece, right_op[index], preferred_element_type=jnp.float32
         ).astype(jnp.bfloat16)
-        right_rows = right_op[index]
         return acc + jnp.einsum(
-            "vacik,ckl->vacil", left_part, right_rows, preferred_element_type=jnp.float32
+            "aij,vacjl->vacil", lefts[index], mid, preferred_element_type=jnp.float32
         )
 
     partial_value = lax.fori_loop(0, terms, one_term, empty)
@@ -37,8 +236,10 @@
 
 
 def solution(mesh):
+    sizes = dict(mesh.shape)
+    small = sizes["sec"] == 4 and sizes["ops"] == 2 and sizes["sub"] == 2
     return jax.shard_map(
-        local,
+        local_small if small else local_any,
         mesh=mesh,
         in_specs=(
             P("runs", "sec", None, None, "sub"),

time: 97.4 us -> 31.4 us (0.32)
  the two profiles are of different devices: /device:TPU:0 before, /device:TPU:28 now
where the time goes in v2:
time: 31.4 us; the launch traced here: 31.3 us
  waiting for transfers between devices  13.7 us (44%)
  starting transfers between devices  11.7 us (37%)
  Pallas kernels  3.68 us (12%)
  local copies, waits for them, and re-layouts  1.87 us (6%)
    ppermute x12, waiting for transfers between devices, in_pieces(): lax.ppermute(part, axis_name, swap)  5.15 us
    ppermute x3, waiting for transfers between devices, exchange(): return lax.ppermute(value, 'sec', [(z, z ^ offset) for z in range(sectors)])  4.57 us
    ppermute x4, starting transfers between devices, in_pieces(): return lax.ppermute(value, axis_name, swap)  4.09 us
    ppermute x12, starting transfers between devices, in_pieces(): lax.ppermute(part, axis_name, swap)  3.99 us
    ppermute x4, waiting for transfers between devices, in_pieces(): return lax.ppermute(value, axis_name, swap)  3.95 us
    ppermute x3, starting transfers between devices, exchange(): return lax.ppermute(value, 'sec', [(z, z ^ offset) for z in range(sectors)])  3.62 us
    pallas_call x3, Pallas kernels, blocks_call(): pl.pallas_call(kernel, out_shape=(jax.ShapeDtypeStruct(shape, jnp.bfloat1...  2.89 us
    reshape x1, local copies, waits for them, and re-layouts, pick(): return block.reshape(1, block_rows, half_cols)  1.09 us
  transfers between devices with their start and end apart: 19, of which 10 were waited for; matrix products, arithmetic and copies ran while one was open for 1% of the time, Pallas kernels for 9%

profile of v2, /device:TPU:28, one launch (start us, length us, event | category | flops | bytes accessed | tf_op | source)
XLA Modules:
  0.0 31.3 jit_solution(7547963728308137323)
XLA Ops:
  0.0 0.0 copy-start.1
  0.0 1.1 %dynamic-slice_bitcast_fusion = (bf16[1,128,256]{2,1,0:T(8,128)(2,1)S(1)}, bf16[1,128,256]{2,1,0:T(8,128)(2,1)S(1)}, bf16[1,128,256]{2,1,0:T(8,128)(2,1)S(1)}, b...) fusion(bf16[2,1,4,128,256]{4,3,2,1,0:T(8,128)(2,1)} %param.5, ...), kind=kLoop, calls=%fused_computation.16 | loop fusion | bytes 917524 | tf_op jit(solution)/shard_map/reshape | solution.py:171
  1.1 0.0 copy-done.1
  1.2 0.0 copy-start
  1.2 0.5 %collective-permute-start.2 = (bf16[3,128,256]{2,1,0:T(8,128)(2,1)S(1)}, bf16[3,128,256]{2,1,0:T(8,128)(2,1)S(1)}, u32[]{:S(2)}, u32[]{:S(2)}) collective-permute-start(bf16[3,128,256]{2,1,0:T(8,128)(2,1)S(1)} %get-tuple-element.69), channel_id=1, source_target_pairs={{0,4},{4,0},{8,12},{12,8},{1,5},{5,1},{9,13},{13,9},{2,6},{6,2},{1... | collective-permute-start | bytes 589832 | tf_op jit(solution)/shard_map/ppermute | solution.py:155
  1.7 0.0 collective-permute-start
  1.7 0.5 %collective-permute-start.1 = (bf16[128,256]{1,0:T(8,128)(2,1)S(1)}, bf16[128,256]{1,0:T(8,128)(2,1)S(1)}, u32[]{:S(2)}, u32[]{:S(2)}) collective-permute-start(bf16[128,256]{1,0:T(8,128)(2,1)S(1)} %bitcast.58), channel_id=1, source_target_pairs={{0,1},{1,0},{2,3},{3,2},{4,5},{5,4},{6,7},{7,6},{8,9},{9,8},{10,11... | collective-permute-start | bytes 196616 | tf_op jit(solution)/shard_map/ppermute | solution.py:162
  2.3 1.4 %collective-permute-start.6 = (bf16[2,128,256]{2,1,0:T(8,128)(2,1)S(1)}, bf16[2,128,256]{2,1,0:T(8,128)(2,1)S(1)}, u32[]{:S(2)}, u32[]{:S(2)}) collective-permute-start(bf16[2,128,256]{2,1,0:T(8,128)(2,1)S(1)} %pad_maximum_fusion.6), channel_id=1, source_target_pairs={{0,12},{4,8},{8,4},{12,0},{1,13},{5,9},{9,5},{13,1},{2,14},{6,10},... | collective-permute-start | bytes 393224 | tf_op jit(solution)/shard_map/ppermute | solution.py:155
  3.7 1.7 %collective-permute-start.14 = (bf16[3,128,256]{2,1,0:T(8,128)(2,1)S(1)}, bf16[3,128,256]{2,1,0:T(8,128)(2,1)S(1)}, u32[]{:S(2)}, u32[]{:S(2)}) collective-permute-start(bf16[3,128,256]{2,1,0:T(8,128)(2,1)S(1)} %get-tuple-element.68), channel_id=1, source_target_pairs={{0,8},{4,12},{8,0},{12,4},{1,9},{5,13},{9,1},{13,5},{2,10},{6,14},... | collective-permute-start | bytes 589832 | tf_op jit(solution)/shard_map/ppermute | solution.py:155
  5.4 4.6 %collective-permute-done.2.near = bf16[3,128,256]{2,1,0:T(8,128)(2,1)S(1)} collective-permute-done((bf16[3,128,256]{2,1,0:T(8,128)(2,1)S(1)}, bf16[3,128,256]{2,1,0:T(8,128)(2,1)S(1)}, u32[]{:S(2)}, u32[]{:S(2)}) %collective-permute-start.2) | collective-permute-done | bytes 196640 | tf_op jit(solution)/shard_map/ppermute | solution.py:155
  10.0 0.1 collective-permute-start.3
  10.0 0.0 collective-permute-done
  10.1 0.5 %collective-permute-start.4 = (bf16[128,256]{1,0:T(8,128)(2,1)S(1)}, bf16[128,256]{1,0:T(8,128)(2,1)S(1)}, u32[]{:S(2)}, u32[]{:S(2)}) collective-permute-start(bf16[128,256]{1,0:T(8,128)(2,1)S(1)} %get-tuple-element.58), channel_id=1, source_target_pairs={{0,1},{1,0},{2,3},{3,2},{4,5},{5,4},{6,7},{7,6},{8,9},{9,8},{10,11... | collective-permute-start | bytes 196616 | tf_op jit(solution)/shard_map/ppermute | solution.py:162
  10.5 0.0 collective-permute-done.1
  10.5 0.1 collective-permute-start.5
  10.6 0.6 %collective-permute-done.3 = bf16[128,256]{1,0:T(8,128)(2,1)S(1)} collective-permute-done((bf16[128,256]{1,0:T(8,128)(2,1)S(1)}, bf16[128,256]{1,0:T(8,128)(2,1)S(1)}, u32[]{:S(2)}, u32[]{:S(2)}) %collective-permute-start.3) | collective-permute-done | bytes 65568 | tf_op jit(solution)/shard_map/ppermute | solution.py:162
  11.3 0.2 collective-permute-done.4
  11.4 0.4 %collective-permute-done.5 = bf16[128,256]{1,0:T(8,128)(2,1)S(1)} collective-permute-done((bf16[128,256]{1,0:T(8,128)(2,1)S(1)}, bf16[128,256]{1,0:T(8,128)(2,1)S(1)}, u32[]{:S(2)}, u32[]{:S(2)}) %collective-permute-start.5) | collective-permute-done | bytes 65568 | tf_op jit(solution)/shard_map/ppermute | solution.py:162
  11.8 0.0 copy-start.2
  11.8 0.0 copy-start.3
  11.8 0.0 copy-done
  11.9 0.7 %copy-done.2 = s32[4,4]{1,0:T(4,128)S(1)} copy-done((s32[4,4]{1,0:T(4,128)S(1)}, s32[4,4]{1,0:T(4,128)}, u32[]{:S(2)}) %copy-start.2) | copy-done | bytes 88
  12.5 0.0 copy-done.3
  12.5 1.6 %shard_map.55 = (bf16[2,2,64,256]{3,2,1,0:T(8,128)(2,1)S(1)}, f32[2,2,64,256]{3,2,1,0:T(8,128)S(1)}, s32[4,8,128]{2,1,0:T(8,128)S(1)}, s32[4,8,128]{2,1,0:T(8,128)S(1)}) custom-call(s32[4]{0:T(128)S(1)} %copy-done.3, s32[4,4]{1,0:T(4,128)S(1)} %copy-done.2, bf16[4,512,256]{2,1,0:T(8,128)(2,1)S(1)} %bitcast.47, bf16[4,128,128]{2,1,0:T(8,128)(2,1)S(1)} %bitcast.55, ...), custom_call_target="tpu_custom_call" | custom-call | tf_op jit(solution)/shard_map/pallas_call | solution.py:107
  14.2 1.6 %collective-permute-start.8 = (bf16[128,256]{1,0:T(8,128)(2,1)S(1)}, bf16[128,256]{1,0:T(8,128)(2,1)S(1)}, u32[]{:S(2)}, u32[]{:S(2)}) collective-permute-start(bf16[128,256]{1,0:T(8,128)(2,1)S(1)} %bitcast.62), channel_id=1, source_target_pairs={{0,2},{2,0},{1,3},{3,1},{4,6},{6,4},{5,7},{7,5},{8,10},{10,8},{9,1... | collective-permute-start | bytes 196616 | tf_op jit(solution)/shard_map/ppermute | solution.py:162
  15.7 0.5 %collective-permute-start.9 = (bf16[128,256]{1,0:T(8,128)(2,1)S(1)}, bf16[128,256]{1,0:T(8,128)(2,1)S(1)}, u32[]{:S(2)}, u32[]{:S(2)}) collective-permute-start(bf16[128,256]{1,0:T(8,128)(2,1)S(1)} %bitcast.60), channel_id=1, source_target_pairs={{0,2},{2,0},{1,3},{3,1},{4,6},{6,4},{5,7},{7,5},{8,10},{10,8},{9,1... | collective-permute-start | bytes 196616 | tf_op jit(solution)/shard_map/ppermute | solution.py:162
  16.3 0.0 collective-permute-done.6
  16.3 1.6 %collective-permute-start.7 = (bf16[1,128,256]{2,1,0:T(8,128)(2,1)S(1)}, bf16[1,128,256]{2,1,0:T(8,128)(2,1)S(1)}, u32[]{:S(2)}, u32[]{:S(2)}) collective-permute-start(bf16[1,128,256]{2,1,0:T(8,128)(2,1)S(1)} %get-tuple-element.61), channel_id=1, source_target_pairs={{0,2},{2,0},{1,3},{3,1},{4,6},{6,4},{5,7},{7,5},{8,10},{10,8},{9,1... | collective-permute-start | bytes 196616 | tf_op jit(solution)/shard_map/ppermute | solution.py:159
  17.8 0.0 collective-permute-start.10
  17.8 1.0 %collective-permute-done.8 = bf16[128,256]{1,0:T(8,128)(2,1)S(1)} collective-permute-done((bf16[128,256]{1,0:T(8,128)(2,1)S(1)}, bf16[128,256]{1,0:T(8,128)(2,1)S(1)}, u32[]{:S(2)}, u32[]{:S(2)}) %collective-permute-start.8) | collective-permute-done | bytes 65568 | tf_op jit(solution)/shard_map/ppermute | solution.py:162
  18.9 0.0 collective-permute-start.12
  18.9 1.7 %collective-permute-done.9 = bf16[128,256]{1,0:T(8,128)(2,1)S(1)} collective-permute-done((bf16[128,256]{1,0:T(8,128)(2,1)S(1)}, bf16[128,256]{1,0:T(8,128)(2,1)S(1)}, u32[]{:S(2)}, u32[]{:S(2)}) %collective-permute-start.9) | collective-permute-done | bytes 65568 | tf_op jit(solution)/shard_map/ppermute | solution.py:162
  20.6 0.7 %collective-permute-done.7 = bf16[1,128,256]{2,1,0:T(8,128)(2,1)S(1)} collective-permute-done((bf16[1,128,256]{2,1,0:T(8,128)(2,1)S(1)}, bf16[1,128,256]{2,1,0:T(8,128)(2,1)S(1)}, u32[]{:S(2)}, u32[]{:S(2)}) %collective-permute-start.7) | collective-permute-done | bytes 65568 | tf_op jit(solution)/shard_map/ppermute | solution.py:159
  21.3 0.0 collective-permute-start.11
  21.3 0.0 collective-permute-done.10
  21.3 1.2 %collective-permute-done.11 = bf16[128,256]{1,0:T(8,128)(2,1)S(1)} collective-permute-done((bf16[128,256]{1,0:T(8,128)(2,1)S(1)}, bf16[128,256]{1,0:T(8,128)(2,1)S(1)}, u32[]{:S(2)}, u32[]{:S(2)}) %collective-permute-start.11) | collective-permute-done | bytes 65568 | tf_op jit(solution)/shard_map/ppermute | solution.py:162
  22.6 0.0 collective-permute-done.12.refs_3_
  22.6 0.6 %shard_map.56 = (bf16[1,2,64,256]{3,2,1,0:T(8,128)(2,1)S(1)}, f32[1,2,64,256]{3,2,1,0:T(8,128)S(1)}) custom-call(s32[4,8,128]{2,1,0:T(8,128)S(1)} %get-tuple-element.34.used_ref, bf16[4,512,256]{2,1,0:T(8,128)(2,1)S(1)} %bitcast.48, bf16[2,128,256]{2,1,0:T(8,128)(2,1)S(1)} %pad_maximum_fusion.8.refs_0_, bf16[2,128,256]{2,1,0:T(8,128)(2,1)S(1)} %bitcast.53, ...), custom_call_target="tpu_custom_call" | custom-call | tf_op jit(solution)/shard_map/pallas_call | solution.py:107
  23.2 0.0 collective-permute-done.14.refs_0_
  23.3 0.2 collective-permute-start.15
  23.5 0.4 %collective-permute-start.16 = (bf16[128,256]{1,0:T(8,128)(2,1)S(1)}, bf16[128,256]{1,0:T(8,128)(2,1)S(1)}, u32[]{:S(2)}, u32[]{:S(2)}) collective-permute-start(bf16[128,256]{1,0:T(8,128)(2,1)S(1)} %get-tuple-element.54), channel_id=1, source_target_pairs={{0,1},{1,0},{2,3},{3,2},{4,5},{5,4},{6,7},{7,6},{8,9},{9,8},{10,11... | collective-permute-start | bytes 196616 | tf_op jit(solution)/shard_map/ppermute | solution.py:162
  23.8 0.2 collective-permute-start.17
  24.0 1.5 %collective-permute-start.13 = (bf16[1,2,64,256]{3,2,1,0:T(8,128)(2,1)S(1)}, bf16[1,2,64,256]{3,2,1,0:T(8,128)(2,1)S(1)}, u32[]{:S(2)}, u32[]{:S(2)}) collective-permute-start(bf16[1,2,64,256]{3,2,1,0:T(8,128)(2,1)S(1)} %get-tuple-element.37), channel_id=1, source_target_pairs={{0,2},{2,0},{1,3},{3,1},{4,6},{6,4},{5,7},{7,5},{8,10},{10,8},{9,1... | collective-permute-start | bytes 196616 | tf_op jit(solution)/shard_map/ppermute | solution.py:159
  25.5 0.0 collective-permute-done.15
  25.5 0.0 collective-permute-done.16
  25.5 0.0 collective-permute-done.17
  25.5 0.6 %shard_map.57 = (bf16[1,2,64,256]{3,2,1,0:T(8,128)(2,1)S(1)}, f32[1,2,64,256]{3,2,1,0:T(8,128)S(1)}) custom-call(s32[4,8,128]{2,1,0:T(8,128)S(1)} %get-tuple-element.34.used_ref, bf16[4,512,256]{2,1,0:T(8,128)(2,1)S(1)} %bitcast.49, bf16[3,128,256]{2,1,0:T(8,128)(2,1)S(1)} %collective-permute-done.14.refs_0_, bf16[3,128,256]{2,1,0:T(8,128)(2,1)S(1)} %bitcast.51, ...), custom_call_target="tpu_custom_call" | custom-call | tf_op jit(solution)/shard_map/pallas_call | solution.py:107
  26.1 1.1 %collective-permute-start.18 = (bf16[1,2,64,256]{3,2,1,0:T(8,128)(2,1)S(1)}, bf16[1,2,64,256]{3,2,1,0:T(8,128)(2,1)S(1)}, u32[]{:S(2)}, u32[]{:S(2)}) collective-permute-start(bf16[1,2,64,256]{3,2,1,0:T(8,128)(2,1)S(1)} %get-tuple-element.42), channel_id=1, source_target_pairs={{0,2},{2,0},{1,3},{3,1},{4,6},{6,4},{5,7},{7,5},{8,10},{10,8},{9,1... | collective-permute-start | bytes 196616 | tf_op jit(solution)/shard_map/ppermute | solution.py:159
  27.2 1.2 %collective-permute-done.13.got_b = bf16[1,2,64,256]{3,2,1,0:T(8,128)(2,1)S(1)} collective-permute-done((bf16[1,2,64,256]{3,2,1,0:T(8,128)(2,1)S(1)}, bf16[1,2,64,256]{3,2,1,0:T(8,128)(2,1)S(1)}, u32[]{:S(2)}, u32[]{:S(2)}) %collective-permute-start.13) | collective-permute-done | bytes 65568 | tf_op jit(solution)/shard_map/ppermute | solution.py:159
  28.4 2.0 %collective-permute-done.18.got_c = bf16[1,2,64,256]{3,2,1,0:T(8,128)(2,1)S(1)} collective-permute-done((bf16[1,2,64,256]{3,2,1,0:T(8,128)(2,1)S(1)}, bf16[1,2,64,256]{3,2,1,0:T(8,128)(2,1)S(1)}, u32[]{:S(2)}, u32[]{:S(2)}) %collective-permute-start.18) | collective-permute-done | bytes 65568 | tf_op jit(solution)/shard_map/ppermute | solution.py:159
  30.5 0.8 %shard_map.58 = bf16[2,4,1,64,256]{4,3,2,1,0:T(8,128)(2,1)} custom-call(s32[4,8,128]{2,1,0:T(8,128)S(1)} %get-tuple-element.29.shown_ref, f32[1,2,64,256]{3,2,1,0:T(8,128)S(1)} %get-tuple-element.51.keep_m, bf16[1,2,64,256]{3,2,1,0:T(8,128)(2,1)S(1)} %get-tuple-element.63.got_m, f32[1,2,64,256]{3,2,1,0:T(8,128)S(1)} %get-tuple-element.50.keep_n, ...), custom_call_target="tpu_custom_call" | custom-call | tf_op jit(solution)/shard_map/pallas_call | solution.py:138
  (17 shorter events, 0.2 us)
Async XLA Ops:
  0.0 1.1 %copy-start.1 = (bf16[4,1,128,128]{3,2,1,0:T(8,128)(2,1)S(1)}, bf16[4,1,128,128]{3,2,1,0:T(8,128)(2,1)}, u32[]{:S(2)}) copy-start(bf16[4,1,128,128]{3,2,1,0:T(8,128)(2,1)} %param.6) | copy-start | bytes 393220
  1.2 10.7 %copy-start = (bf16[4,1,512,256]{3,2,1,0:T(8,128)(2,1)S(1)}, bf16[4,1,512,256]{3,2,1,0:T(8,128)(2,1)}, u32[]{:S(2)}) copy-start(bf16[4,1,512,256]{3,2,1,0:T(8,128)(2,1)} %param.7) | copy-start | bytes 3145732
  1.2 8.7 %collective-permute-start.2 = (bf16[3,128,256]{2,1,0:T(8,128)(2,1)S(1)}, bf16[3,128,256]{2,1,0:T(8,128)(2,1)S(1)}, u32[]{:S(2)}, u32[]{:S(2)}) collective-permute-start(bf16[3,128,256]{2,1,0:T(8,128)(2,1)S(1)} %get-tuple-element.69), channel_id=1, source_target_pairs={{0,4},{4,0},{8,12},{12,8},{1,5},{5,1},{9,13},{13,9},{2,6},{6,2},{1... | collective-permute-start | bytes 589832 | tf_op jit(solution)/shard_map/ppermute | solution.py:155
  1.7 8.3 %collective-permute-start = (bf16[128,256]{1,0:T(8,128)(2,1)S(1)}, bf16[128,256]{1,0:T(8,128)(2,1)S(1)}, u32[]{:S(2)}, u32[]{:S(2)}) collective-permute-start(bf16[128,256]{1,0:T(8,128)(2,1)S(1)} %bitcast.59), channel_id=1, source_target_pairs={{0,1},{1,0},{2,3},{3,2},{4,5},{5,4},{6,7},{7,6},{8,9},{9,8},{10,11... | collective-permute-start | bytes 196616 | tf_op jit(solution)/shard_map/ppermute | solution.py:162
  1.7 8.8 %collective-permute-start.1 = (bf16[128,256]{1,0:T(8,128)(2,1)S(1)}, bf16[128,256]{1,0:T(8,128)(2,1)S(1)}, u32[]{:S(2)}, u32[]{:S(2)}) collective-permute-start(bf16[128,256]{1,0:T(8,128)(2,1)S(1)} %bitcast.58), channel_id=1, source_target_pairs={{0,1},{1,0},{2,3},{3,2},{4,5},{5,4},{6,7},{7,6},{8,9},{9,8},{10,11... | collective-permute-start | bytes 196616 | tf_op jit(solution)/shard_map/ppermute | solution.py:162
  2.3 14.0 %collective-permute-start.6 = (bf16[2,128,256]{2,1,0:T(8,128)(2,1)S(1)}, bf16[2,128,256]{2,1,0:T(8,128)(2,1)S(1)}, u32[]{:S(2)}, u32[]{:S(2)}) collective-permute-start(bf16[2,128,256]{2,1,0:T(8,128)(2,1)S(1)} %pad_maximum_fusion.6), channel_id=1, source_target_pairs={{0,12},{4,8},{8,4},{12,0},{1,13},{5,9},{9,5},{13,1},{2,14},{6,10},... | collective-permute-start | bytes 393224 | tf_op jit(solution)/shard_map/ppermute | solution.py:155
  3.7 19.5 %collective-permute-start.14 = (bf16[3,128,256]{2,1,0:T(8,128)(2,1)S(1)}, bf16[3,128,256]{2,1,0:T(8,128)(2,1)S(1)}, u32[]{:S(2)}, u32[]{:S(2)}) collective-permute-start(bf16[3,128,256]{2,1,0:T(8,128)(2,1)S(1)} %get-tuple-element.68), channel_id=1, source_target_pairs={{0,8},{4,12},{8,0},{12,4},{1,9},{5,13},{9,1},{13,5},{2,10},{6,14},... | collective-permute-start | bytes 589832 | tf_op jit(solution)/shard_map/ppermute | solution.py:155
  10.0 1.3 %collective-permute-start.3 = (bf16[128,256]{1,0:T(8,128)(2,1)S(1)}, bf16[128,256]{1,0:T(8,128)(2,1)S(1)}, u32[]{:S(2)}, u32[]{:S(2)}) collective-permute-start(bf16[128,256]{1,0:T(8,128)(2,1)S(1)} %get-tuple-element.56), channel_id=1, source_target_pairs={{0,1},{1,0},{2,3},{3,2},{4,5},{5,4},{6,7},{7,6},{8,9},{9,8},{10,11... | collective-permute-start | bytes 196616 | tf_op jit(solution)/shard_map/ppermute | solution.py:162
  10.1 1.4 %collective-permute-start.4 = (bf16[128,256]{1,0:T(8,128)(2,1)S(1)}, bf16[128,256]{1,0:T(8,128)(2,1)S(1)}, u32[]{:S(2)}, u32[]{:S(2)}) collective-permute-start(bf16[128,256]{1,0:T(8,128)(2,1)S(1)} %get-tuple-element.58), channel_id=1, source_target_pairs={{0,1},{1,0},{2,3},{3,2},{4,5},{5,4},{6,7},{7,6},{8,9},{9,8},{10,11... | collective-permute-start | bytes 196616 | tf_op jit(solution)/shard_map/ppermute | solution.py:162
  10.5 1.3 %collective-permute-start.5 = (bf16[128,256]{1,0:T(8,128)(2,1)S(1)}, bf16[128,256]{1,0:T(8,128)(2,1)S(1)}, u32[]{:S(2)}, u32[]{:S(2)}) collective-permute-start(bf16[128,256]{1,0:T(8,128)(2,1)S(1)} %get-tuple-element.57), channel_id=1, source_target_pairs={{0,1},{1,0},{2,3},{3,2},{4,5},{5,4},{6,7},{7,6},{8,9},{9,8},{10,11... | collective-permute-start | bytes 196616 | tf_op jit(solution)/shard_map/ppermute | solution.py:162
  11.8 0.7 %copy-start.2 = (s32[4,4]{1,0:T(4,128)S(1)}, s32[4,4]{1,0:T(4,128)}, u32[]{:S(2)}) copy-start(s32[4,4]{1,0:T(4,128)} %live_ref.1) | copy-start | bytes 196
  11.8 0.7 %copy-start.3 = (s32[4]{0:T(128)S(1)}, s32[4]{0:T(128)}, u32[]{:S(2)}) copy-start(s32[4]{0:T(128)} %rows_ref.1) | copy-start | bytes 52
  14.2 4.7 %collective-permute-start.8 = (bf16[128,256]{1,0:T(8,128)(2,1)S(1)}, bf16[128,256]{1,0:T(8,128)(2,1)S(1)}, u32[]{:S(2)}, u32[]{:S(2)}) collective-permute-start(bf16[128,256]{1,0:T(8,128)(2,1)S(1)} %bitcast.62), channel_id=1, source_target_pairs={{0,2},{2,0},{1,3},{3,1},{4,6},{6,4},{5,7},{7,5},{8,10},{10,8},{9,1... | collective-permute-start | bytes 196616 | tf_op jit(solution)/shard_map/ppermute | solution.py:162
  15.7 4.9 %collective-permute-start.9 = (bf16[128,256]{1,0:T(8,128)(2,1)S(1)}, bf16[128,256]{1,0:T(8,128)(2,1)S(1)}, u32[]{:S(2)}, u32[]{:S(2)}) collective-permute-start(bf16[128,256]{1,0:T(8,128)(2,1)S(1)} %bitcast.60), channel_id=1, source_target_pairs={{0,2},{2,0},{1,3},{3,1},{4,6},{6,4},{5,7},{7,5},{8,10},{10,8},{9,1... | collective-permute-start | bytes 196616 | tf_op jit(solution)/shard_map/ppermute | solution.py:162
  16.3 5.0 %collective-permute-start.7 = (bf16[1,128,256]{2,1,0:T(8,128)(2,1)S(1)}, bf16[1,128,256]{2,1,0:T(8,128)(2,1)S(1)}, u32[]{:S(2)}, u32[]{:S(2)}) collective-permute-start(bf16[1,128,256]{2,1,0:T(8,128)(2,1)S(1)} %get-tuple-element.61), channel_id=1, source_target_pairs={{0,2},{2,0},{1,3},{3,1},{4,6},{6,4},{5,7},{7,5},{8,10},{10,8},{9,1... | collective-permute-start | bytes 196616 | tf_op jit(solution)/shard_map/ppermute | solution.py:159
  17.8 3.5 %collective-permute-start.10 = (bf16[128,256]{1,0:T(8,128)(2,1)S(1)}, bf16[128,256]{1,0:T(8,128)(2,1)S(1)}, u32[]{:S(2)}, u32[]{:S(2)}) collective-permute-start(bf16[128,256]{1,0:T(8,128)(2,1)S(1)} %get-tuple-element.60), channel_id=1, source_target_pairs={{0,1},{1,0},{2,3},{3,2},{4,5},{5,4},{6,7},{7,6},{8,9},{9,8},{10,11... | collective-permute-start | bytes 196616 | tf_op jit(solution)/shard_map/ppermute | solution.py:162
  18.9 3.7 %collective-permute-start.12 = (bf16[1,128,256]{2,1,0:T(8,128)(2,1)S(1)}, bf16[1,128,256]{2,1,0:T(8,128)(2,1)S(1)}, u32[]{:S(2)}, u32[]{:S(2)}) collective-permute-start(bf16[1,128,256]{2,1,0:T(8,128)(2,1)S(1)} %get-tuple-element.59.refs_2_), channel_id=1, source_target_pairs={{0,1},{1,0},{2,3},{3,2},{4,5},{5,4},{6,7},{7,6},{8,9},{9,8},{10,11... | collective-permute-start | bytes 196616 | tf_op jit(solution)/shard_map/ppermute | solution.py:159
  21.3 1.3 %collective-permute-start.11 = (bf16[128,256]{1,0:T(8,128)(2,1)S(1)}, bf16[128,256]{1,0:T(8,128)(2,1)S(1)}, u32[]{:S(2)}, u32[]{:S(2)}) collective-permute-start(bf16[128,256]{1,0:T(8,128)(2,1)S(1)} %bitcast.61), channel_id=1, source_target_pairs={{0,1},{1,0},{2,3},{3,2},{4,5},{5,4},{6,7},{7,6},{8,9},{9,8},{10,11... | collective-permute-start | bytes 196616 | tf_op jit(solution)/shard_map/ppermute | solution.py:162
  23.3 2.2 %collective-permute-start.15 = (bf16[128,256]{1,0:T(8,128)(2,1)S(1)}, bf16[128,256]{1,0:T(8,128)(2,1)S(1)}, u32[]{:S(2)}, u32[]{:S(2)}) collective-permute-start(bf16[128,256]{1,0:T(8,128)(2,1)S(1)} %get-tuple-element.55), channel_id=1, source_target_pairs={{0,1},{1,0},{2,3},{3,2},{4,5},{5,4},{6,7},{7,6},{8,9},{9,8},{10,11... | collective-permute-start | bytes 196616 | tf_op jit(solution)/shard_map/ppermute | solution.py:162
  23.5 2.0 %collective-permute-start.16 = (bf16[128,256]{1,0:T(8,128)(2,1)S(1)}, bf16[128,256]{1,0:T(8,128)(2,1)S(1)}, u32[]{:S(2)}, u32[]{:S(2)}) collective-permute-start(bf16[128,256]{1,0:T(8,128)(2,1)S(1)} %get-tuple-element.54), channel_id=1, source_target_pairs={{0,1},{1,0},{2,3},{3,2},{4,5},{5,4},{6,7},{7,6},{8,9},{9,8},{10,11... | collective-permute-start | bytes 196616 | tf_op jit(solution)/shard_map/ppermute | solution.py:162
  23.8 1.6 %collective-permute-start.17 = (bf16[128,256]{1,0:T(8,128)(2,1)S(1)}, bf16[128,256]{1,0:T(8,128)(2,1)S(1)}, u32[]{:S(2)}, u32[]{:S(2)}) collective-permute-start(bf16[128,256]{1,0:T(8,128)(2,1)S(1)} %get-tuple-element.53), channel_id=1, source_target_pairs={{0,1},{1,0},{2,3},{3,2},{4,5},{5,4},{6,7},{7,6},{8,9},{9,8},{10,11... | collective-permute-start | bytes 196616 | tf_op jit(solution)/shard_map/ppermute | solution.py:162
  24.0 4.4 %collective-permute-start.13 = (bf16[1,2,64,256]{3,2,1,0:T(8,128)(2,1)S(1)}, bf16[1,2,64,256]{3,2,1,0:T(8,128)(2,1)S(1)}, u32[]{:S(2)}, u32[]{:S(2)}) collective-permute-start(bf16[1,2,64,256]{3,2,1,0:T(8,128)(2,1)S(1)} %get-tuple-element.37), channel_id=1, source_target_pairs={{0,2},{2,0},{1,3},{3,1},{4,6},{6,4},{5,7},{7,5},{8,10},{10,8},{9,1... | collective-permute-start | bytes 196616 | tf_op jit(solution)/shard_map/ppermute | solution.py:159
  26.1 4.3 %collective-permute-start.18 = (bf16[1,2,64,256]{3,2,1,0:T(8,128)(2,1)S(1)}, bf16[1,2,64,256]{3,2,1,0:T(8,128)(2,1)S(1)}, u32[]{:S(2)}, u32[]{:S(2)}) collective-permute-start(bf16[1,2,64,256]{3,2,1,0:T(8,128)(2,1)S(1)} %get-tuple-element.42), channel_id=1, source_target_pairs={{0,2},{2,0},{1,3},{3,1},{4,6},{6,4},{5,7},{7,5},{8,10},{10,8},{9,1... | collective-permute-start | bytes 196616 | tf_op jit(solution)/shard_map/ppermute | solution.py:159

commit v3 on v2

--- a/solution.py
+++ b/solution.py
@@ -8,7 +8,6 @@
 from jax.sharding import PartitionSpec as P
 
 VMEM = pl.BlockSpec(memory_space=pltpu.VMEM)
-SMEM = pl.BlockSpec(memory_space=pltpu.SMEM)
 
 
 def wide_left(low, high, rows):
@@ -18,7 +17,7 @@
     return jnp.where(column < rows, wide, jnp.zeros_like(wide))
 
 
-def sector_product(mine, other, right, wide, half):
+def right_product(mine, other, right, half):
     vectors, block_rows, half_cols = mine.shape
     terms = right.shape[0]
     x_mine = mine.reshape(vectors * block_rows, half_cols)
@@ -30,11 +29,13 @@
         value = jnp.dot(x_mine, near_rows, preferred_element_type=jnp.float32)
         value = value + jnp.dot(x_other, far_rows, preferred_element_type=jnp.float32)
         mid.append(value.astype(jnp.bfloat16).reshape(vectors, block_rows, -1))
-    out = []
-    for vector in range(vectors):
-        tall = jnp.concatenate([mid[term][vector] for term in range(terms)], axis=0)
-        out.append(jnp.dot(wide, tall, preferred_element_type=jnp.float32))
-    return out
+    return [
+        jnp.concatenate([mid[term][vector] for term in range(terms)], axis=0) for vector in range(vectors)
+    ]
+
+
+def left_product(wide, tall):
+    return [jnp.dot(wide, value, preferred_element_type=jnp.float32) for value in tall]
 
 
 def store_halves(values, own, send_ref, keep_ref, slot):
@@ -53,10 +54,19 @@
     return jnp.where(own == 0, values[0], values[1]), jnp.where(own == 0, values[1], values[0])
 
 
-def own_kernel(rows_ref, live_ref, right, left, mine, other, send_ref, keep_ref, used_ref, shown_ref):
+def own_kernel(rows_hbm, live_hbm, right, left, mine, other,
+               send_ref, keep_ref, used_ref, shown_ref, rows_ref, live_ref, sems):
     me, own, half = lax.axis_index("sec"), lax.axis_index("ops"), lax.axis_index("sub")
-    sectors = rows_ref.shape[0]
-    for offset in range(sectors):
+    copies = [
+        pltpu.make_async_copy(rows_hbm, rows_ref, sems.at[0]),
+        pltpu.make_async_copy(live_hbm, live_ref, sems.at[1]),
+    ]
+    for copy in copies:
+        copy.start()
+    tall = right_product(mine[...], other[...], right, half)
+    for copy in copies:
+        copy.wait()
+    for offset in range(rows_ref.shape[0]):
         sector = me ^ offset
         used = rows_ref[sector]
         used_ref[offset] = jnp.full(used_ref.shape[1:], used, jnp.int32)
@@ -65,30 +75,23 @@
         )
     low = jnp.concatenate([left[0], left[1]], axis=1)
     high = jnp.concatenate([left[2], left[3]], axis=1)
-    values = sector_product(mine[...], other[...], right, wide_left(low, high, rows_ref[me]), half)
+    values = left_product(wide_left(low, high, rows_ref[me]), tall)
     store_halves(values, own, send_ref, keep_ref, 0)
 
 
-def near_kernel(used_ref, right, near, other, send_ref, keep_ref):
-    own, half = lax.axis_index("ops"), lax.axis_index("sub")
-    wide = wide_left(*halves(near[2], other[2], half), used_ref[1, :1, :1])
-    values = sector_product(near[:2], other[:2], right, wide, half)
-    store_halves(values, own, send_ref, keep_ref, 0)
-
-
-def early_kernel(rows_ref, live_ref, right, left, mine, other, near, near_other,
-                 send_ref, keep_ref, used_ref, shown_ref):
-    own_kernel(rows_ref, live_ref, right, left, mine, other, send_ref.at[:1], keep_ref.at[:1], used_ref, shown_ref)
-    near_kernel(used_ref, right, near, near_other, send_ref.at[1:], keep_ref.at[1:])
-
-
-def far_kernel(plan, used_ref, right, *refs):
+def block_kernel(plan, used_ref, right, *refs):
     own, half = lax.axis_index("ops"), lax.axis_index("sub")
     send_ref, keep_ref = refs[-2:]
     for number, (offset, own_order) in enumerate(plan):
         psi, other, left, left_other = refs[4 * number:4 * number + 4]
-        wide = wide_left(*halves(left[0], left_other[0], half), used_ref[offset, :1, :1])
-        values = sector_product(psi[:2], other[:2], right, wide, half)
+        tall = right_product(psi[:2], other[:2], right, half)
+        if left.shape[0] == 1:
+            sides = halves(left[0], left_other[0], half)
+        else:
+            whole = [jnp.where(half == offset - 2, left[term], left_other[term]) for term in range(4)]
+            sides = jnp.concatenate(whole[:2], axis=1), jnp.concatenate(whole[2:], axis=1)
+        wide = wide_left(*sides, used_ref[offset, :1, :1])
+        values = left_product(wide, tall)
         if own_order:
             values = by_vector(values, own)
         store_halves(values, own, send_ref, keep_ref, number)
@@ -102,8 +105,10 @@
 
 
 def blocks_call(kernel, count, right, *operands, scalars=(), extra=(), us=0):
-    columns = right.shape[2]
-    shape = (count, 2, right.shape[1] // 8, columns)
+    shape = (count, 2, right.shape[1] // 8, right.shape[2])
+    scratch = [pltpu.SMEM(array.shape, array.dtype) for array in scalars]
+    if scalars:
+        scratch.append(pltpu.SemaphoreType.DMA((len(scalars),)))
     return pl.pallas_call(
         kernel,
         out_shape=(
@@ -111,8 +116,9 @@
             jax.ShapeDtypeStruct(shape, jnp.float32),
             *extra,
         ),
-        in_specs=[SMEM] * len(scalars) + [VMEM] * (len(operands)),
+        in_specs=[pl.BlockSpec(memory_space=pltpu.HBM)] * len(scalars) + [VMEM] * len(operands),
         out_specs=(VMEM,) * (2 + len(extra)),
+        scratch_shapes=scratch,
         cost_estimate=cost(us),
         compiler_params=PARAMS,
     )(*scalars, *operands)
@@ -176,30 +182,31 @@
     half_left = jnp.concatenate([half_left[0], half_left[1]], axis=1)[None]
     mine = jnp.concatenate(pieces[:2])
     near = jnp.concatenate([*pieces[2:4], half_left])
-    skip = jnp.concatenate([*pieces[4:6], half_left])
-    cross = jnp.concatenate([*pieces[6:], half_left])
+    skip = jnp.concatenate([*pieces[4:6]])
+    cross = jnp.concatenate([*pieces[6:]])
     rows_shape = jax.ShapeDtypeStruct((sectors, 8, 128), jnp.int32)
+    far_pairs = [(2 * z + s, 2 * (z ^ (2 + s)) + s) for z in range(4) for s in range(2)]
+    cross_left = skip_left = lax.ppermute(left, ("sec", "sub"), far_pairs)
     near_in = exchange(near, 1)
     cross_in = exchange(cross, 3)
     skip_in = exchange(skip, 2)
-    mine_other = other_core(mine, 2)
-    near_other = other_core(near_in, 3)
-    send_a, keep_a, used, shown = blocks_call(early_kernel, 2, right, right, left, mine, mine_other, near_in, near_other, scalars=(sector_rows, block_live), extra=(rows_shape, rows_shape), us=0)
-    got_a = in_pieces(send_a, "ops", 2)
-    cross_left = cross_in[1:]
+    cross_left_other = skip_left_other = in_pieces(cross_left, "sub", 1)
+    mine_other = other_core(mine, 1)
+    near_other = other_core(near_in, 2)
+    send_m, keep_m, used, shown = blocks_call(own_kernel, 1, right, right, left, mine, mine_other, scalars=(sector_rows, block_live), extra=(rows_shape, rows_shape), us=0)
+    send_n, keep_n = blocks_call(functools.partial(block_kernel, ((1, False),)), 1, right, used, right, near_in, near_other, near_in[2:], near_other[2:], us=0)
+    got_m = in_pieces(send_m, "ops", 2)
+    got_n = in_pieces(send_n, "ops", 1)
+    cross_in, got_m = lax.optimization_barrier((cross_in, got_m))
     cross_swapped = in_pieces(cross_in[:1], "ops", 1)
-    cross_swapped, got_a = lax.optimization_barrier((cross_swapped, got_a))
     cross_psi = jnp.concatenate([cross_in[:1], cross_swapped])
     cross_other = other_core(cross_psi, 2)
-    cross_left_other = other_core(cross_left, 1)
-    send_b, keep_b = blocks_call(functools.partial(far_kernel, ((3, True),)), 1, right, used, right, cross_psi, cross_other, cross_left, cross_left_other, us=0)
+    send_b, keep_b = blocks_call(functools.partial(block_kernel, ((3, True),)), 1, right, used, right, cross_psi, cross_other, cross_left, cross_left_other, us=0)
     got_b = in_pieces(send_b, "ops", 1)
     skip_in, send_b = lax.optimization_barrier((skip_in, send_b))
-    skip_other = other_core(skip_in, 3)
-    skip_left, skip_left_other = skip_in[2:], skip_other[2:]
-    send_c, keep_c = blocks_call(functools.partial(far_kernel, ((2, False),)), 1, right, used, right, skip_in, skip_other, skip_left, skip_left_other, us=0)
+    skip_other = other_core(skip_in, 1)
+    send_c, keep_c = blocks_call(functools.partial(block_kernel, ((2, False),)), 1, right, used, right, skip_in, skip_other, skip_left, skip_left_other, us=0)
     got_c = in_pieces(send_c, "ops", 1)
-    keep_m, keep_n, got_m, got_n = keep_a[:1], keep_a[1:], got_a[:1], got_a[1:]
     shape = (vectors, sectors, sec_dev, block_rows // 2, half_cols)
     return final_call(shown, (keep_m, got_m, keep_n, got_n, keep_b, got_b, keep_c, got_c), shape)
 

time: 31.4 us -> 29.4 us (0.936)
  the two profiles are of different devices: /device:TPU:28 before, /device:TPU:0 now
where the time goes in v3:
time: 29.4 us; the launch traced here: 29.2 us
  starting transfers between devices  13.5 us (46%)
  waiting for transfers between devices  10.7 us (36%)
  Pallas kernels  3.51 us (12%)
  local copies, waits for them, and re-layouts  1.14 us (4%)
    ppermute x7, waiting for transfers between devices, in_pieces(): return lax.ppermute(value, axis_name, swap)  4.37 us
    ppermute x1, starting transfers between devices, local_small(): cross_left = skip_left = lax.ppermute(left, ('sec', 'sub'), far_pairs)  4.04 us
    ppermute x7, starting transfers between devices, in_pieces(): return lax.ppermute(value, axis_name, swap)  3.9 us
    ppermute x3, starting transfers between devices, exchange(): return lax.ppermute(value, 'sec', [(z, z ^ offset) for z in range(sectors)])  2.81 us
    ppermute x6, starting transfers between devices, in_pieces(): lax.ppermute(part, axis_name, swap)  2.79 us
    pallas_call x4, Pallas kernels, blocks_call(): pl.pallas_call(kernel, out_shape=(jax.ShapeDtypeStruct(shape, jnp.bfloat1...  2.72 us
    ppermute x3, waiting for transfers between devices, exchange(): return lax.ppermute(value, 'sec', [(z, z ^ offset) for z in range(sectors)])  2.7 us
    ppermute x6, waiting for transfers between devices, in_pieces(): lax.ppermute(part, axis_name, swap)  1.83 us
  transfers between devices with their start and end apart: 17, of which 8 were waited for; matrix products, arithmetic and copies ran while one was open for 4% of the time, Pallas kernels for 9%

profile of v3, /device:TPU:0, one launch (start us, length us, event | category | flops | bytes accessed | tf_op | source)
XLA Modules:
  0.0 29.2 jit_solution(17429356905976459752)
XLA Ops:
  0.0 0.0 copy-start
  0.0 4.0 %collective-permute-start.11 = (bf16[4,128,128]{2,1,0:T(8,128)(2,1)}, bf16[4,128,128]{2,1,0:T(8,128)(2,1)S(1)}, u32[]{:S(2)}, u32[]{:S(2)}) collective-permute-start(bf16[4,128,128]{2,1,0:T(8,128)(2,1)} %bitcast.41), channel_id=1, source_target_pairs={{0,8},{1,13},{4,12},{5,9},{8,0},{9,5},{12,4},{13,1},{2,10},{3,15},... | collective-permute-start | bytes 393224 | tf_op jit(solution)/shard_map/ppermute | solution.py:189
  4.0 1.1 %dynamic-slice_bitcast_fusion = (bf16[1,128,256]{2,1,0:T(8,128)(2,1)S(1)}, bf16[1,128,256]{2,1,0:T(8,128)(2,1)S(1)}, bf16[1,128,256]{2,1,0:T(8,128)(2,1)S(1)}, b...) fusion(bf16[2,1,4,128,256]{4,3,2,1,0:T(8,128)(2,1)} %param.5, ...), kind=kLoop, calls=%fused_computation.8 | loop fusion | bytes 917524 | tf_op jit(solution)/shard_map/reshape | solution.py:177
  5.1 0.0 copy-start.1
  5.1 1.4 %collective-permute-start.1 = (bf16[1,128,256]{2,1,0:T(8,128)(2,1)S(1)}, bf16[1,128,256]{2,1,0:T(8,128)(2,1)S(1)}, u32[]{:S(2)}, u32[]{:S(2)}) collective-permute-start(bf16[1,128,256]{2,1,0:T(8,128)(2,1)S(1)} %get-tuple-element.30), channel_id=1, source_target_pairs={{0,12},{4,8},{8,4},{12,0},{1,13},{5,9},{9,5},{13,1},{2,14},{6,10},... | collective-permute-start | bytes 196616 | tf_op jit(solution)/shard_map/ppermute | solution.py:161
  6.5 0.1 collective-permute-start
  6.6 0.0 copy-done.1
  6.7 0.0 copy-start.2
  6.7 0.0 copy-start.3
  6.7 1.0 %collective-permute-start.4 = (bf16[3,128,256]{2,1,0:T(8,128)(2,1)S(1)}, bf16[3,128,256]{2,1,0:T(8,128)(2,1)S(1)}, u32[]{:S(2)}, u32[]{:S(2)}) collective-permute-start(bf16[3,128,256]{2,1,0:T(8,128)(2,1)S(1)} %pad_maximum_fusion), channel_id=1, source_target_pairs={{0,4},{4,0},{8,12},{12,8},{1,5},{5,1},{9,13},{13,9},{2,6},{6,2},{1... | collective-permute-start | bytes 589832 | tf_op jit(solution)/shard_map/ppermute | solution.py:161
  7.7 0.2 collective-permute-done.other
  8.0 0.0 copy-done
  8.0 0.0 copy-done.2
  8.0 0.0 copy-done.3
  8.0 0.9 %shard_map.55 = (bf16[1,2,64,256]{3,2,1,0:T(8,128)(2,1)S(1)}, f32[1,2,64,256]{3,2,1,0:T(8,128)S(1)}, s32[4,8,128]{2,1,0:T(8,128)S(1)}, s32[4,8,128]{2,1,0:T(8,128)S(1)}) custom-call(s32[4]{0:T(128)S(1)} %copy-done.3, s32[4,4]{1,0:T(4,128)S(1)} %copy-done.2, bf16[4,512,256]{2,1,0:T(8,128)(2,1)S(1)} %bitcast.34, bf16[4,128,128]{2,1,0:T(8,128)(2,1)S(1)} %bitcast.43, ...), custom_call_target="tpu_custom_call" | custom-call | tf_op jit(solution)/shard_map/pallas_call | solution.py:112
  8.8 1.6 %collective-permute-start.2 = (bf16[64,256]{1,0:T(8,128)(2,1)S(1)}, bf16[64,256]{1,0:T(8,128)(2,1)S(1)}, u32[]{:S(2)}, u32[]{:S(2)}) collective-permute-start(bf16[64,256]{1,0:T(8,128)(2,1)S(1)} %get-tuple-element.58), channel_id=1, source_target_pairs={{0,2},{2,0},{1,3},{3,1},{4,6},{6,4},{5,7},{7,5},{8,10},{10,8},{9,1... | collective-permute-start | bytes 98312 | tf_op jit(solution)/shard_map/ppermute | solution.py:168
  10.4 0.5 %collective-permute-start.3 = (bf16[64,256]{1,0:T(8,128)(2,1)S(1)}, bf16[64,256]{1,0:T(8,128)(2,1)S(1)}, u32[]{:S(2)}, u32[]{:S(2)}) collective-permute-start(bf16[64,256]{1,0:T(8,128)(2,1)S(1)} %get-tuple-element.59), channel_id=1, source_target_pairs={{0,2},{2,0},{1,3},{3,1},{4,6},{6,4},{5,7},{7,5},{8,10},{10,8},{9,1... | collective-permute-start | bytes 98312 | tf_op jit(solution)/shard_map/ppermute | solution.py:168
  11.0 1.8 %collective-permute-done.11.refs_2_ = bf16[4,128,128]{2,1,0:T(8,128)(2,1)S(1)} collective-permute-done((bf16[4,128,128]{2,1,0:T(8,128)(2,1)}, bf16[4,128,128]{2,1,0:T(8,128)(2,1)S(1)}, u32[]{:S(2)}, u32[]{:S(2)}) %collective-permute-start.11) | collective-permute-done | bytes 131104 | tf_op jit(solution)/shard_map/ppermute | solution.py:189
  12.8 0.4 %collective-permute-start.14 = (bf16[2,128,256]{2,1,0:T(8,128)(2,1)S(1)}, bf16[2,128,256]{2,1,0:T(8,128)(2,1)S(1)}, u32[]{:S(2)}, u32[]{:S(2)}) collective-permute-start(bf16[2,128,256]{2,1,0:T(8,128)(2,1)S(1)} %pad_maximum_fusion.4), channel_id=1, source_target_pairs={{0,8},{4,12},{8,0},{12,4},{1,9},{5,13},{9,1},{13,5},{2,10},{6,14},... | collective-permute-start | bytes 393224 | tf_op jit(solution)/shard_map/ppermute | solution.py:161
  13.2 0.0 collective-permute-done.2
  13.2 0.0 collective-permute-start.12
  13.2 1.2 %collective-permute-done.3 = bf16[64,256]{1,0:T(8,128)(2,1)S(1)} collective-permute-done((bf16[64,256]{1,0:T(8,128)(2,1)S(1)}, bf16[64,256]{1,0:T(8,128)(2,1)S(1)}, u32[]{:S(2)}, u32[]{:S(2)}) %collective-permute-start.3) | collective-permute-done | bytes 32800 | tf_op jit(solution)/shard_map/ppermute | solution.py:168
  14.3 0.0 collective-permute-done.1
  14.4 0.6 %collective-permute-start.8 = (bf16[1,128,256]{2,1,0:T(8,128)(2,1)S(1)}, bf16[1,128,256]{2,1,0:T(8,128)(2,1)S(1)}, u32[]{:S(2)}, u32[]{:S(2)}) collective-permute-start(bf16[1,128,256]{2,1,0:T(8,128)(2,1)S(1)} %collective-permute-done.1), channel_id=1, source_target_pairs={{0,2},{2,0},{1,3},{3,1},{4,6},{6,4},{5,7},{7,5},{8,10},{10,8},{9,1... | collective-permute-start | bytes 196616 | tf_op jit(solution)/shard_map/ppermute | solution.py:165
  14.9 0.1 collective-permute-start.9
  15.0 2.7 %collective-permute-done.4.refs_0_ = bf16[3,128,256]{2,1,0:T(8,128)(2,1)S(1)} collective-permute-done((bf16[3,128,256]{2,1,0:T(8,128)(2,1)S(1)}, bf16[3,128,256]{2,1,0:T(8,128)(2,1)S(1)}, u32[]{:S(2)}, u32[]{:S(2)}) %collective-permute-start.4) | collective-permute-done | bytes 196640 | tf_op jit(solution)/shard_map/ppermute | solution.py:161
  17.7 0.1 collective-permute-start.5
  17.8 0.9 %collective-permute-done.8 = bf16[1,128,256]{2,1,0:T(8,128)(2,1)S(1)} collective-permute-done((bf16[1,128,256]{2,1,0:T(8,128)(2,1)S(1)}, bf16[1,128,256]{2,1,0:T(8,128)(2,1)S(1)}, u32[]{:S(2)}, u32[]{:S(2)}) %collective-permute-start.8) | collective-permute-done | bytes 65568 | tf_op jit(solution)/shard_map/ppermute | solution.py:165
  18.7 0.0 collective-permute-start.10
  18.7 0.0 collective-permute-done.9
  18.7 0.6 %collective-permute-start.6 = (bf16[192,256]{1,0:T(8,128)(2,1)S(1)}, bf16[192,256]{1,0:T(8,128)(2,1)S(1)}, u32[]{:S(2)}, u32[]{:S(2)}) collective-permute-start(bf16[192,256]{1,0:T(8,128)(2,1)S(1)} %get-tuple-element.55), channel_id=1, source_target_pairs={{0,1},{1,0},{2,3},{3,2},{4,5},{5,4},{6,7},{7,6},{8,9},{9,8},{10,11... | collective-permute-start | bytes 294920 | tf_op jit(solution)/shard_map/ppermute | solution.py:168
  19.3 0.7 %collective-permute-done.10 = bf16[128,256]{1,0:T(8,128)(2,1)S(1)} collective-permute-done((bf16[128,256]{1,0:T(8,128)(2,1)S(1)}, bf16[128,256]{1,0:T(8,128)(2,1)S(1)}, u32[]{:S(2)}, u32[]{:S(2)}) %collective-permute-start.10) | collective-permute-done | bytes 65568 | tf_op jit(solution)/shard_map/ppermute | solution.py:168
  20.0 0.0 collective-permute-done.12.refs_3_
  20.0 0.6 %shard_map.57 = (bf16[1,2,64,256]{3,2,1,0:T(8,128)(2,1)S(1)}, f32[1,2,64,256]{3,2,1,0:T(8,128)S(1)}) custom-call(s32[4,8,128]{2,1,0:T(8,128)S(1)} %get-tuple-element.33.used_ref, bf16[4,512,256]{2,1,0:T(8,128)(2,1)S(1)} %bitcast.35, bf16[2,128,256]{2,1,0:T(8,128)(2,1)S(1)} %pad_maximum_fusion.2.refs_0_, bf16[2,128,256]{2,1,0:T(8,128)(2,1)S(1)} %bitcast.40, ...), custom_call_target="tpu_custom_call" | custom-call | tf_op jit(solution)/shard_map/pallas_call | solution.py:112
  20.6 1.0 %collective-permute-start.13 = (bf16[1,2,64,256]{3,2,1,0:T(8,128)(2,1)S(1)}, bf16[1,2,64,256]{3,2,1,0:T(8,128)(2,1)S(1)}, u32[]{:S(2)}, u32[]{:S(2)}) collective-permute-start(bf16[1,2,64,256]{3,2,1,0:T(8,128)(2,1)S(1)} %get-tuple-element.41), channel_id=1, source_target_pairs={{0,2},{2,0},{1,3},{3,1},{4,6},{6,4},{5,7},{7,5},{8,10},{10,8},{9,1... | collective-permute-start | bytes 196616 | tf_op jit(solution)/shard_map/ppermute | solution.py:165
  21.6 0.0 collective-permute-done.14.refs_0_
  21.6 0.1 collective-permute-start.15
  21.7 0.0 collective-permute-done.6
  21.7 0.0 collective-permute-done.5
  21.7 0.6 %shard_map.56 = (bf16[1,2,64,256]{3,2,1,0:T(8,128)(2,1)S(1)}, f32[1,2,64,256]{3,2,1,0:T(8,128)S(1)}) custom-call(s32[4,8,128]{2,1,0:T(8,128)S(1)} %get-tuple-element.33.used_ref, bf16[4,512,256]{2,1,0:T(8,128)(2,1)S(1)} %bitcast.36, bf16[3,128,256]{2,1,0:T(8,128)(2,1)S(1)} %collective-permute-done.4.refs_0_, bf16[3,128,256]{2,1,0:T(8,128)(2,1)S(1)} %bitcast.39, ...), custom_call_target="tpu_custom_call" | custom-call | tf_op jit(solution)/shard_map/pallas_call | solution.py:112
  22.4 1.1 %collective-permute-start.7 = (bf16[1,2,64,256]{3,2,1,0:T(8,128)(2,1)S(1)}, bf16[1,2,64,256]{3,2,1,0:T(8,128)(2,1)S(1)}, u32[]{:S(2)}, u32[]{:S(2)}) collective-permute-start(bf16[1,2,64,256]{3,2,1,0:T(8,128)(2,1)S(1)} %get-tuple-element.38), channel_id=1, source_target_pairs={{0,2},{2,0},{1,3},{3,1},{4,6},{6,4},{5,7},{7,5},{8,10},{10,8},{9,1... | collective-permute-start | bytes 196616 | tf_op jit(solution)/shard_map/ppermute | solution.py:165
  23.5 0.0 collective-permute-done.15.refs_1_
  23.5 0.6 %shard_map.58 = (bf16[1,2,64,256]{3,2,1,0:T(8,128)(2,1)S(1)}, f32[1,2,64,256]{3,2,1,0:T(8,128)S(1)}) custom-call(s32[4,8,128]{2,1,0:T(8,128)S(1)} %get-tuple-element.33.used_ref, bf16[4,512,256]{2,1,0:T(8,128)(2,1)S(1)} %bitcast.37, bf16[2,128,256]{2,1,0:T(8,128)(2,1)S(1)} %collective-permute-done.14.refs_0_, ...), custom_call_target="tpu_custom_call" | custom-call | tf_op jit(solution)/shard_map/pallas_call | solution.py:112
  24.1 1.1 %collective-permute-start.16 = (bf16[1,2,64,256]{3,2,1,0:T(8,128)(2,1)S(1)}, bf16[1,2,64,256]{3,2,1,0:T(8,128)(2,1)S(1)}, u32[]{:S(2)}, u32[]{:S(2)}) collective-permute-start(bf16[1,2,64,256]{3,2,1,0:T(8,128)(2,1)S(1)} %get-tuple-element.46), channel_id=1, source_target_pairs={{0,2},{2,0},{1,3},{3,1},{4,6},{6,4},{5,7},{7,5},{8,10},{10,8},{9,1... | collective-permute-start | bytes 196616 | tf_op jit(solution)/shard_map/ppermute | solution.py:165
  25.2 0.0 collective-permute-done.13.got_b
  25.2 1.7 %collective-permute-done.7.got_n = bf16[1,2,64,256]{3,2,1,0:T(8,128)(2,1)S(1)} collective-permute-done((bf16[1,2,64,256]{3,2,1,0:T(8,128)(2,1)S(1)}, bf16[1,2,64,256]{3,2,1,0:T(8,128)(2,1)S(1)}, u32[]{:S(2)}, u32[]{:S(2)}) %collective-permute-start.7) | collective-permute-done | bytes 65568 | tf_op jit(solution)/shard_map/ppermute | solution.py:165
  26.9 1.5 %collective-permute-done.16.got_c = bf16[1,2,64,256]{3,2,1,0:T(8,128)(2,1)S(1)} collective-permute-done((bf16[1,2,64,256]{3,2,1,0:T(8,128)(2,1)S(1)}, bf16[1,2,64,256]{3,2,1,0:T(8,128)(2,1)S(1)}, u32[]{:S(2)}, u32[]{:S(2)}) %collective-permute-start.16) | collective-permute-done | bytes 65568 | tf_op jit(solution)/shard_map/ppermute | solution.py:165
  28.4 0.8 %shard_map.59 = bf16[2,4,1,64,256]{4,3,2,1,0:T(8,128)(2,1)} custom-call(s32[4,8,128]{2,1,0:T(8,128)S(1)} %get-tuple-element.28.shown_ref, f32[1,2,64,256]{3,2,1,0:T(8,128)S(1)} %get-tuple-element.29.keep_m, bf16[1,2,64,256]{3,2,1,0:T(8,128)(2,1)S(1)} %bitcast.44, f32[1,2,64,256]{3,2,1,0:T(8,128)S(1)} %get-tuple-element.37.keep_n, ...), custom_call_target="tpu_custom_call" | custom-call | tf_op jit(solution)/shard_map/pallas_call | solution.py:144
  (14 shorter events, 0.1 us)
Async XLA Ops:
  0.0 8.0 %copy-start = (bf16[4,1,512,256]{3,2,1,0:T(8,128)(2,1)S(1)}, bf16[4,1,512,256]{3,2,1,0:T(8,128)(2,1)}, u32[]{:S(2)}) copy-start(bf16[4,1,512,256]{3,2,1,0:T(8,128)(2,1)} %param.7) | copy-start | bytes 3145732
  0.0 12.8 %collective-permute-start.11 = (bf16[4,128,128]{2,1,0:T(8,128)(2,1)}, bf16[4,128,128]{2,1,0:T(8,128)(2,1)S(1)}, u32[]{:S(2)}, u32[]{:S(2)}) collective-permute-start(bf16[4,128,128]{2,1,0:T(8,128)(2,1)} %bitcast.41), channel_id=1, source_target_pairs={{0,8},{1,13},{4,12},{5,9},{8,0},{9,5},{12,4},{13,1},{2,10},{3,15},... | collective-permute-start | bytes 393224 | tf_op jit(solution)/shard_map/ppermute | solution.py:189
  5.1 1.5 %copy-start.1 = (bf16[4,1,128,128]{3,2,1,0:T(8,128)(2,1)S(1)}, bf16[4,1,128,128]{3,2,1,0:T(8,128)(2,1)}, u32[]{:S(2)}) copy-start(bf16[4,1,128,128]{3,2,1,0:T(8,128)(2,1)} %param.6) | copy-start | bytes 393220
  5.1 9.2 %collective-permute-start.1 = (bf16[1,128,256]{2,1,0:T(8,128)(2,1)S(1)}, bf16[1,128,256]{2,1,0:T(8,128)(2,1)S(1)}, u32[]{:S(2)}, u32[]{:S(2)}) collective-permute-start(bf16[1,128,256]{2,1,0:T(8,128)(2,1)S(1)} %get-tuple-element.30), channel_id=1, source_target_pairs={{0,12},{4,8},{8,4},{12,0},{1,13},{5,9},{9,5},{13,1},{2,14},{6,10},... | collective-permute-start | bytes 196616 | tf_op jit(solution)/shard_map/ppermute | solution.py:161
  6.5 1.4 %collective-permute-start = (bf16[2,128,256]{2,1,0:T(8,128)(2,1)S(1)}, bf16[2,128,256]{2,1,0:T(8,128)(2,1)S(1)}, u32[]{:S(2)}, u32[]{:S(2)}) collective-permute-start(bf16[2,128,256]{2,1,0:T(8,128)(2,1)S(1)} %constant_dynamic-update-slice_fusion.mine), channel_id=1, source_target_pairs={{0,1},{1,0},{2,3},{3,2},{4,5},{5,4},{6,7},{7,6},{8,9},{9,8},{10,11... | collective-permute-start | bytes 393224 | tf_op jit(solution)/shard_map/ppermute | solution.py:165
  6.7 1.3 %copy-start.2 = (s32[4,4]{1,0:T(4,128)S(1)}, s32[4,4]{1,0:T(4,128)}, u32[]{:S(2)}) copy-start(s32[4,4]{1,0:T(4,128)} %live_hbm.1) | copy-start | bytes 196
  6.7 1.2 %copy-start.3 = (s32[4]{0:T(128)S(1)}, s32[4]{0:T(128)}, u32[]{:S(2)}) copy-start(s32[4]{0:T(128)} %rows_hbm.1) | copy-start | bytes 52
  6.7 10.9 %collective-permute-start.4 = (bf16[3,128,256]{2,1,0:T(8,128)(2,1)S(1)}, bf16[3,128,256]{2,1,0:T(8,128)(2,1)S(1)}, u32[]{:S(2)}, u32[]{:S(2)}) collective-permute-start(bf16[3,128,256]{2,1,0:T(8,128)(2,1)S(1)} %pad_maximum_fusion), channel_id=1, source_target_pairs={{0,4},{4,0},{8,12},{12,8},{1,5},{5,1},{9,13},{13,9},{2,6},{6,2},{1... | collective-permute-start | bytes 589832 | tf_op jit(solution)/shard_map/ppermute | solution.py:161
  8.8 4.3 %collective-permute-start.2 = (bf16[64,256]{1,0:T(8,128)(2,1)S(1)}, bf16[64,256]{1,0:T(8,128)(2,1)S(1)}, u32[]{:S(2)}, u32[]{:S(2)}) collective-permute-start(bf16[64,256]{1,0:T(8,128)(2,1)S(1)} %get-tuple-element.58), channel_id=1, source_target_pairs={{0,2},{2,0},{1,3},{3,1},{4,6},{6,4},{5,7},{7,5},{8,10},{10,8},{9,1... | collective-permute-start | bytes 98312 | tf_op jit(solution)/shard_map/ppermute | solution.py:168
  10.4 3.9 %collective-permute-start.3 = (bf16[64,256]{1,0:T(8,128)(2,1)S(1)}, bf16[64,256]{1,0:T(8,128)(2,1)S(1)}, u32[]{:S(2)}, u32[]{:S(2)}) collective-permute-start(bf16[64,256]{1,0:T(8,128)(2,1)S(1)} %get-tuple-element.59), channel_id=1, source_target_pairs={{0,2},{2,0},{1,3},{3,1},{4,6},{6,4},{5,7},{7,5},{8,10},{10,8},{9,1... | collective-permute-start | bytes 98312 | tf_op jit(solution)/shard_map/ppermute | solution.py:168
  12.8 8.9 %collective-permute-start.14 = (bf16[2,128,256]{2,1,0:T(8,128)(2,1)S(1)}, bf16[2,128,256]{2,1,0:T(8,128)(2,1)S(1)}, u32[]{:S(2)}, u32[]{:S(2)}) collective-permute-start(bf16[2,128,256]{2,1,0:T(8,128)(2,1)S(1)} %pad_maximum_fusion.4), channel_id=1, source_target_pairs={{0,8},{4,12},{8,0},{12,4},{1,9},{5,13},{9,1},{13,5},{2,10},{6,14},... | collective-permute-start | bytes 393224 | tf_op jit(solution)/shard_map/ppermute | solution.py:161
  13.2 6.8 %collective-permute-start.12 = (bf16[4,128,128]{2,1,0:T(8,128)(2,1)S(1)}, bf16[4,128,128]{2,1,0:T(8,128)(2,1)S(1)}, u32[]{:S(2)}, u32[]{:S(2)}) collective-permute-start(bf16[4,128,128]{2,1,0:T(8,128)(2,1)S(1)} %collective-permute-done.11.refs_2_), channel_id=1, source_target_pairs={{0,1},{1,0},{2,3},{3,2},{4,5},{5,4},{6,7},{7,6},{8,9},{9,8},{10,11... | collective-permute-start | bytes 393224 | tf_op jit(solution)/shard_map/ppermute | solution.py:165
  14.4 4.3 %collective-permute-start.8 = (bf16[1,128,256]{2,1,0:T(8,128)(2,1)S(1)}, bf16[1,128,256]{2,1,0:T(8,128)(2,1)S(1)}, u32[]{:S(2)}, u32[]{:S(2)}) collective-permute-start(bf16[1,128,256]{2,1,0:T(8,128)(2,1)S(1)} %collective-permute-done.1), channel_id=1, source_target_pairs={{0,2},{2,0},{1,3},{3,1},{4,6},{6,4},{5,7},{7,5},{8,10},{10,8},{9,1... | collective-permute-start | bytes 196616 | tf_op jit(solution)/shard_map/ppermute | solution.py:165
  14.9 3.8 %collective-permute-start.9 = (bf16[128,256]{1,0:T(8,128)(2,1)S(1)}, bf16[128,256]{1,0:T(8,128)(2,1)S(1)}, u32[]{:S(2)}, u32[]{:S(2)}) collective-permute-start(bf16[128,256]{1,0:T(8,128)(2,1)S(1)} %bitcast.45), channel_id=1, source_target_pairs={{0,1},{1,0},{2,3},{3,2},{4,5},{5,4},{6,7},{7,6},{8,9},{9,8},{10,11... | collective-permute-start | bytes 196616 | tf_op jit(solution)/shard_map/ppermute | solution.py:168
  17.7 4.0 %collective-permute-start.5 = (bf16[192,256]{1,0:T(8,128)(2,1)S(1)}, bf16[192,256]{1,0:T(8,128)(2,1)S(1)}, u32[]{:S(2)}, u32[]{:S(2)}) collective-permute-start(bf16[192,256]{1,0:T(8,128)(2,1)S(1)} %get-tuple-element.54), channel_id=1, source_target_pairs={{0,1},{1,0},{2,3},{3,2},{4,5},{5,4},{6,7},{7,6},{8,9},{9,8},{10,11... | collective-permute-start | bytes 294920 | tf_op jit(solution)/shard_map/ppermute | solution.py:168
  18.7 1.3 %collective-permute-start.10 = (bf16[128,256]{1,0:T(8,128)(2,1)S(1)}, bf16[128,256]{1,0:T(8,128)(2,1)S(1)}, u32[]{:S(2)}, u32[]{:S(2)}) collective-permute-start(bf16[128,256]{1,0:T(8,128)(2,1)S(1)} %bitcast.46), channel_id=1, source_target_pairs={{0,1},{1,0},{2,3},{3,2},{4,5},{5,4},{6,7},{7,6},{8,9},{9,8},{10,11... | collective-permute-start | bytes 196616 | tf_op jit(solution)/shard_map/ppermute | solution.py:168
  18.7 3.0 %collective-permute-start.6 = (bf16[192,256]{1,0:T(8,128)(2,1)S(1)}, bf16[192,256]{1,0:T(8,128)(2,1)S(1)}, u32[]{:S(2)}, u32[]{:S(2)}) collective-permute-start(bf16[192,256]{1,0:T(8,128)(2,1)S(1)} %get-tuple-element.55), channel_id=1, source_target_pairs={{0,1},{1,0},{2,3},{3,2},{4,5},{5,4},{6,7},{7,6},{8,9},{9,8},{10,11... | collective-permute-start | bytes 294920 | tf_op jit(solution)/shard_map/ppermute | solution.py:168
  20.6 4.6 %collective-permute-start.13 = (bf16[1,2,64,256]{3,2,1,0:T(8,128)(2,1)S(1)}, bf16[1,2,64,256]{3,2,1,0:T(8,128)(2,1)S(1)}, u32[]{:S(2)}, u32[]{:S(2)}) collective-permute-start(bf16[1,2,64,256]{3,2,1,0:T(8,128)(2,1)S(1)} %get-tuple-element.41), channel_id=1, source_target_pairs={{0,2},{2,0},{1,3},{3,1},{4,6},{6,4},{5,7},{7,5},{8,10},{10,8},{9,1... | collective-permute-start | bytes 196616 | tf_op jit(solution)/shard_map/ppermute | solution.py:165
  21.6 1.8 %collective-permute-start.15 = (bf16[2,128,256]{2,1,0:T(8,128)(2,1)S(1)}, bf16[2,128,256]{2,1,0:T(8,128)(2,1)S(1)}, u32[]{:S(2)}, u32[]{:S(2)}) collective-permute-start(bf16[2,128,256]{2,1,0:T(8,128)(2,1)S(1)} %collective-permute-done.14.refs_0_), channel_id=1, source_target_pairs={{0,1},{1,0},{2,3},{3,2},{4,5},{5,4},{6,7},{7,6},{8,9},{9,8},{10,11... | collective-permute-start | bytes 393224 | tf_op jit(solution)/shard_map/ppermute | solution.py:165
  22.4 4.5 %collective-permute-start.7 = (bf16[1,2,64,256]{3,2,1,0:T(8,128)(2,1)S(1)}, bf16[1,2,64,256]{3,2,1,0:T(8,128)(2,1)S(1)}, u32[]{:S(2)}, u32[]{:S(2)}) collective-permute-start(bf16[1,2,64,256]{3,2,1,0:T(8,128)(2,1)S(1)} %get-tuple-element.38), channel_id=1, source_target_pairs={{0,2},{2,0},{1,3},{3,1},{4,6},{6,4},{5,7},{7,5},{8,10},{10,8},{9,1... | collective-permute-start | bytes 196616 | tf_op jit(solution)/shard_map/ppermute | solution.py:165
  24.1 4.3 %collective-permute-start.16 = (bf16[1,2,64,256]{3,2,1,0:T(8,128)(2,1)S(1)}, bf16[1,2,64,256]{3,2,1,0:T(8,128)(2,1)S(1)}, u32[]{:S(2)}, u32[]{:S(2)}) collective-permute-start(bf16[1,2,64,256]{3,2,1,0:T(8,128)(2,1)S(1)} %get-tuple-element.46), channel_id=1, source_target_pairs={{0,2},{2,0},{1,3},{3,1},{4,6},{6,4},{5,7},{7,5},{8,10},{10,8},{9,1... | collective-permute-start | bytes 196616 | tf_op jit(solution)/shard_map/ppermute | solution.py:165

commit v4 on v3

--- a/solution.py
+++ b/solution.py
@@ -48,10 +48,6 @@
 
 def halves(mine, other, half):
     return jnp.where(half == 0, mine, other), jnp.where(half == 0, other, mine)
-
-
-def by_vector(values, own):
-    return jnp.where(own == 0, values[0], values[1]), jnp.where(own == 0, values[1], values[0])
 
 
 def own_kernel(rows_hbm, live_hbm, right, left, mine, other,
@@ -79,22 +75,21 @@
     store_halves(values, own, send_ref, keep_ref, 0)
 
 
-def block_kernel(plan, used_ref, right, *refs):
+def near_kernel(used_ref, right, near, other, send_ref, keep_ref):
     own, half = lax.axis_index("ops"), lax.axis_index("sub")
-    send_ref, keep_ref = refs[-2:]
-    for number, (offset, own_order) in enumerate(plan):
-        psi, other, left, left_other = refs[4 * number:4 * number + 4]
-        tall = right_product(psi[:2], other[:2], right, half)
-        if left.shape[0] == 1:
-            sides = halves(left[0], left_other[0], half)
-        else:
-            whole = [jnp.where(half == offset - 2, left[term], left_other[term]) for term in range(4)]
-            sides = jnp.concatenate(whole[:2], axis=1), jnp.concatenate(whole[2:], axis=1)
-        wide = wide_left(*sides, used_ref[offset, :1, :1])
-        values = left_product(wide, tall)
-        if own_order:
-            values = by_vector(values, own)
-        store_halves(values, own, send_ref, keep_ref, number)
+    tall = right_product(near[:2], other[:2], right, half)
+    wide = wide_left(*halves(near[2], other[2], half), used_ref[1, :1, :1])
+    store_halves(left_product(wide, tall), own, send_ref, keep_ref, 0)
+
+
+def far_kernel(place, used_ref, right, psi, other, left, left_other, send_ref, keep_ref):
+    own, half = lax.axis_index("ops"), lax.axis_index("sub")
+    number = jnp.where(own == place, 0, 1)
+    tall = right_product(psi[...], other[...], right, half)
+    whole = [jnp.where(half == number, left[term], left_other[term]) for term in range(left.shape[0])]
+    sides = jnp.concatenate(whole[:2], axis=1), jnp.concatenate(whole[2:], axis=1)
+    wide = wide_left(*sides, used_ref[2 + number, :1, :1])
+    store_halves(left_product(wide, tall), own, send_ref, keep_ref, 0)
 
 
 PARAMS = pltpu.CompilerParams(vmem_limit_bytes=24 << 20)
@@ -130,13 +125,13 @@
     row_ids = own * own_rows + lax.broadcasted_iota(jnp.int32, (own_rows, columns), 0)
     pairs = (
         (0, keep_m.at[0], got_m.at[0]), (1, keep_n.at[0], got_n.at[0]),
-        (3, keep_b.at[0], got_b.at[0]), (2, keep_c.at[0], got_c.at[0]),
+        (2 + own, keep_b.at[0], got_c.at[0]), (3 - own, keep_c.at[0], got_b.at[0]),
     )
     for offset, keep_ref, got_ref in pairs:
-        keep = row_ids < shown_ref[offset, :1, :1]
+        shown = row_ids < shown_ref[offset, :1, :1]
         for vector in range(vectors):
             total = keep_ref[vector] + got_ref[vector].astype(jnp.float32)
-            total = jnp.where(keep, total, jnp.zeros_like(total))
+            total = jnp.where(shown, total, jnp.zeros_like(total))
             out_ref[vector, me ^ offset, 0] = total.astype(out_ref.dtype)
 
 
@@ -176,37 +171,37 @@
         )
         return block.reshape(1, block_rows, half_cols)
 
-    pieces = [pick(0, 0), pick(1, 0), pick(0, 1), pick(1, 1), pick(0, 2), pick(1, 2), pick(own, 3)]
+    pieces = [pick(vector, offset) for offset in (0, 1, 2 + own) for vector in range(vectors)]
     left_late, *pieces = lax.optimization_barrier((left, *pieces))
     half_left = lax.dynamic_slice_in_dim(left_late, half * 2, 2, 0)
     half_left = jnp.concatenate([half_left[0], half_left[1]], axis=1)[None]
     mine = jnp.concatenate(pieces[:2])
     near = jnp.concatenate([*pieces[2:4], half_left])
-    skip = jnp.concatenate([*pieces[4:6]])
-    cross = jnp.concatenate([*pieces[6:]])
+    far = jnp.concatenate(pieces[4:])
+
+    def cross(size):
+        return [(2 * z + p, 2 * (z ^ (2 + p)) + p) for z in range(sectors) for p in range(size)]
+
     rows_shape = jax.ShapeDtypeStruct((sectors, 8, 128), jnp.int32)
-    far_pairs = [(2 * z + s, 2 * (z ^ (2 + s)) + s) for z in range(4) for s in range(2)]
-    cross_left = skip_left = lax.ppermute(left, ("sec", "sub"), far_pairs)
+    left_far = lax.ppermute(left, ("sec", "sub"), cross(2))
+    far_in = lax.ppermute(far, ("sec", "ops"), cross(2))
     near_in = exchange(near, 1)
-    cross_in = exchange(cross, 3)
-    skip_in = exchange(skip, 2)
-    cross_left_other = skip_left_other = in_pieces(cross_left, "sub", 1)
     mine_other = other_core(mine, 1)
     near_other = other_core(near_in, 2)
+    left_far_other = in_pieces(left_far, "sub", 2)
     send_m, keep_m, used, shown = blocks_call(own_kernel, 1, right, right, left, mine, mine_other, scalars=(sector_rows, block_live), extra=(rows_shape, rows_shape), us=0)
-    send_n, keep_n = blocks_call(functools.partial(block_kernel, ((1, False),)), 1, right, used, right, near_in, near_other, near_in[2:], near_other[2:], us=0)
-    got_m = in_pieces(send_m, "ops", 2)
+    send_n, keep_n = blocks_call(near_kernel, 1, right, used, right, near_in, near_other, us=5)
+    got_m = in_pieces(send_m, "ops", 1)
     got_n = in_pieces(send_n, "ops", 1)
-    cross_in, got_m = lax.optimization_barrier((cross_in, got_m))
-    cross_swapped = in_pieces(cross_in[:1], "ops", 1)
-    cross_psi = jnp.concatenate([cross_in[:1], cross_swapped])
-    cross_other = other_core(cross_psi, 2)
-    send_b, keep_b = blocks_call(functools.partial(block_kernel, ((3, True),)), 1, right, used, right, cross_psi, cross_other, cross_left, cross_left_other, us=0)
-    got_b = in_pieces(send_b, "ops", 1)
-    skip_in, send_b = lax.optimization_barrier((skip_in, send_b))
-    skip_other = other_core(skip_in, 1)
-    send_c, keep_c = blocks_call(functools.partial(block_kernel, ((2, False),)), 1, right, used, right, skip_in, skip_other, skip_left, skip_left_other, us=0)
-    got_c = in_pieces(send_c, "ops", 1)
+    far_in, got_m = lax.optimization_barrier((far_in, got_m))
+    far_swapped = in_pieces(far_in, "ops", 1)
+    far_other = other_core(far_in, 2)
+    send_b, keep_b = blocks_call(functools.partial(far_kernel, 0), 1, right, used, right, far_in, far_other, left_far, left_far_other, us=2)
+    got_b = lax.ppermute(send_b, "ops", swap)
+    far_swapped, send_b = lax.optimization_barrier((far_swapped, send_b))
+    swapped_other = other_core(far_swapped, 1)
+    send_c, keep_c = blocks_call(functools.partial(far_kernel, 1), 1, right, used, right, far_swapped, swapped_other, left_far, left_far_other, us=0)
+    got_c = lax.ppermute(send_c, "ops", swap)
     shape = (vectors, sectors, sec_dev, block_rows // 2, half_cols)
     return final_call(shown, (keep_m, got_m, keep_n, got_n, keep_b, got_b, keep_c, got_c), shape)
 

time: 29.4 us -> 29.1 us (0.990)
  waiting for transfers between devices: 10.7 us -> 10 us
  starting transfers between devices: 13.5 us -> 13.9 us
    ppermute x1 -> x4, waiting for transfers between devices: 1.81 us -> 6.74 us  [the longest x1 4.11 us: local_small(): left_far = lax.ppermute(left, ('sec', 'sub'), cross(2))]
    ppermute x1 -> x4, starting transfers between devices: 4.04 us -> 7.52 us  [the longest x1 4.04 us: local_small(): left_far = lax.ppermute(left, ('sec', 'sub'), cross(2))]
    ppermute x3 -> x1, waiting for transfers between devices: 2.7 us -> 0.18 us  [exchange(): return lax.ppermute(value, 'sec', [(z, z ^ offset) for z in range(sectors)])]
    ppermute x6, waiting for transfers between devices: 1.83 us -> 0.12 us  [in_pieces(): lax.ppermute(part, axis_name, swap)]
    ppermute x7 -> x5, waiting for transfers between devices: 4.37 us -> 2.96 us  [in_pieces(): return lax.ppermute(value, axis_name, swap)]
    ppermute x3 -> x1, starting transfers between devices: 2.81 us -> 1.64 us  [exchange(): return lax.ppermute(value, 'sec', [(z, z ^ offset) for z in range(sectors)])]
    ppermute x6, starting transfers between devices: 2.79 us -> 1.65 us  [in_pieces(): lax.ppermute(part, axis_name, swap)]
    ppermute x7 -> x5, starting transfers between devices: 3.9 us -> 3.07 us  [in_pieces(): return lax.ppermute(value, axis_name, swap)]
  transfers between devices with their start and end apart: 17 -> 16, of which waited for: 8 -> 7; matrix products, arithmetic and copies ran while one was open for 4% -> 4% of each run, Pallas kernels for 9% -> 9%
where the time goes in v4:
time: 29.1 us; the launch traced here: 28.9 us
  starting transfers between devices  13.9 us (48%)
  waiting for transfers between devices  10 us (34%)
  Pallas kernels  3.5 us (12%)
  local copies, waits for them, and re-layouts  1.26 us (4%)
    ppermute x1, waiting for transfers between devices, local_small(): left_far = lax.ppermute(left, ('sec', 'sub'), cross(2))  4.11 us
    ppermute x1, starting transfers between devices, local_small(): left_far = lax.ppermute(left, ('sec', 'sub'), cross(2))  4.04 us
    ppermute x5, starting transfers between devices, in_pieces(): return lax.ppermute(value, axis_name, swap)  3.07 us
    ppermute x5, waiting for transfers between devices, in_pieces(): return lax.ppermute(value, axis_name, swap)  2.96 us
    pallas_call x4, Pallas kernels, blocks_call(): pl.pallas_call(kernel, out_shape=(jax.ShapeDtypeStruct(shape, jnp.bfloat1...  2.71 us
    ppermute x1, starting transfers between devices, local_small(): got_b = lax.ppermute(send_b, 'ops', swap)  1.98 us
    ppermute x6, starting transfers between devices, in_pieces(): lax.ppermute(part, axis_name, swap)  1.65 us
    ppermute x1, starting transfers between devices, exchange(): return lax.ppermute(value, 'sec', [(z, z ^ offset) for z in range(sectors)])  1.64 us
  transfers between devices with their start and end apart: 16, of which 7 were waited for; matrix products, arithmetic and copies ran while one was open for 4% of the time, Pallas kernels for 9%

profile of v4, /device:TPU:0, one launch (start us, length us, event | category | flops | bytes accessed | tf_op | source)
XLA Modules:
  0.0 28.9 jit_solution(6964957383891225417)
XLA Ops:
  0.0 0.0 copy-start
  0.0 4.0 %collective-permute-start.9 = (bf16[4,128,128]{2,1,0:T(8,128)(2,1)}, bf16[4,128,128]{2,1,0:T(8,128)(2,1)S(1)}, u32[]{:S(2)}, u32[]{:S(2)}) collective-permute-start(bf16[4,128,128]{2,1,0:T(8,128)(2,1)} %bitcast.36), channel_id=1, source_target_pairs={{0,8},{1,13},{4,12},{5,9},{8,0},{9,5},{12,4},{13,1},{2,10},{3,15},... | collective-permute-start | bytes 393224 | tf_op jit(solution)/shard_map/ppermute | solution.py:186
  4.0 1.0 %dynamic-slice_bitcast_fusion = (bf16[1,128,256]{2,1,0:T(8,128)(2,1)S(1)}, bf16[1,128,256]{2,1,0:T(8,128)(2,1)S(1)}, bf16[1,128,256]{2,1,0:T(8,128)(2,1)S(1)}, b...) fusion(bf16[2,1,4,128,256]{4,3,2,1,0:T(8,128)(2,1)} %param.5, ...), kind=kLoop, calls=%fused_computation.8 | loop fusion | bytes 786444 | tf_op jit(solution)/shard_map/reshape | solution.py:172
  5.1 0.0 copy-start.1
  5.1 0.6 %collective-permute-start = (bf16[2,128,256]{2,1,0:T(8,128)(2,1)S(1)}, bf16[2,128,256]{2,1,0:T(8,128)(2,1)S(1)}, u32[]{:S(2)}, u32[]{:S(2)}) collective-permute-start(bf16[2,128,256]{2,1,0:T(8,128)(2,1)S(1)} %constant_dynamic-update-slice_fusion.mine), channel_id=1, source_target_pairs={{0,1},{1,0},{2,3},{3,2},{4,5},{5,4},{6,7},{7,6},{8,9},{9,8},{10,11... | collective-permute-start | bytes 393224 | tf_op jit(solution)/shard_map/ppermute | solution.py:160
  5.8 0.1 collective-permute-start.1
  5.8 0.2 copy-done.1
  6.0 0.0 copy-start.2
  6.1 0.0 copy-start.3
  6.1 1.6 %collective-permute-start.3 = (bf16[3,128,256]{2,1,0:T(8,128)(2,1)S(1)}, bf16[3,128,256]{2,1,0:T(8,128)(2,1)S(1)}, u32[]{:S(2)}, u32[]{:S(2)}) collective-permute-start(bf16[3,128,256]{2,1,0:T(8,128)(2,1)S(1)} %pad_maximum_fusion), channel_id=1, source_target_pairs={{0,4},{4,0},{8,12},{12,8},{1,5},{5,1},{9,13},{13,9},{2,6},{6,2},{1... | collective-permute-start | bytes 589832 | tf_op jit(solution)/shard_map/ppermute | solution.py:156
  7.7 0.0 collective-permute-done.other
  7.7 0.0 copy-done
  7.7 0.0 copy-done.2
  7.7 0.0 copy-done.3
  7.7 0.9 %shard_map.55 = (bf16[1,2,64,256]{3,2,1,0:T(8,128)(2,1)S(1)}, f32[1,2,64,256]{3,2,1,0:T(8,128)S(1)}, s32[4,8,128]{2,1,0:T(8,128)S(1)}, s32[4,8,128]{2,1,0:T(8,128)S(1)}) custom-call(s32[4]{0:T(128)S(1)} %copy-done.3, s32[4,4]{1,0:T(4,128)S(1)} %copy-done.2, bf16[4,512,256]{2,1,0:T(8,128)(2,1)S(1)} %bitcast.30, bf16[4,128,128]{2,1,0:T(8,128)(2,1)S(1)} %bitcast.38, ...), custom_call_target="tpu_custom_call" | custom-call | tf_op jit(solution)/shard_map/pallas_call | solution.py:107
  8.6 1.6 %collective-permute-start.2 = (bf16[1,2,64,256]{3,2,1,0:T(8,128)(2,1)S(1)}, bf16[1,2,64,256]{3,2,1,0:T(8,128)(2,1)S(1)}, u32[]{:S(2)}, u32[]{:S(2)}) collective-permute-start(bf16[1,2,64,256]{3,2,1,0:T(8,128)(2,1)S(1)} %get-tuple-element.31), channel_id=1, source_target_pairs={{0,2},{2,0},{1,3},{3,1},{4,6},{6,4},{5,7},{7,5},{8,10},{10,8},{9,1... | collective-permute-start | bytes 196616 | tf_op jit(solution)/shard_map/ppermute | solution.py:160
  10.2 4.1 %collective-permute-done.9.left = bf16[4,128,128]{2,1,0:T(8,128)(2,1)S(1)} collective-permute-done((bf16[4,128,128]{2,1,0:T(8,128)(2,1)}, bf16[4,128,128]{2,1,0:T(8,128)(2,1)S(1)}, u32[]{:S(2)}, u32[]{:S(2)}) %collective-permute-start.9) | collective-permute-done | bytes 131104 | tf_op jit(solution)/shard_map/ppermute | solution.py:186
  14.3 0.1 collective-permute-start.10
  14.4 0.5 %collective-permute-start.11 = (bf16[256,128]{1,0:T(8,128)(2,1)S(1)}, bf16[256,128]{1,0:T(8,128)(2,1)S(1)}, u32[]{:S(2)}, u32[]{:S(2)}) collective-permute-start(bf16[256,128]{1,0:T(8,128)(2,1)S(1)} %bitcast.42), channel_id=1, source_target_pairs={{0,1},{1,0},{2,3},{3,2},{4,5},{5,4},{6,7},{7,6},{8,9},{9,8},{10,11... | collective-permute-start | bytes 196616 | tf_op jit(solution)/shard_map/ppermute | solution.py:163
  14.9 1.6 %collective-permute-done.1.psi = bf16[2,128,256]{2,1,0:T(8,128)(2,1)S(1)} collective-permute-done((bf16[2,128,256]{2,1,0:T(8,128)(2,1)S(1)}, bf16[2,128,256]{2,1,0:T(8,128)(2,1)S(1)}, u32[]{:S(2)}, u32[]{:S(2)}) %collective-permute-start.1) | collective-permute-done | bytes 131104 | tf_op jit(solution)/shard_map/ppermute | solution.py:187
  16.4 0.0 collective-permute-done.2.got_m
  16.5 0.2 collective-permute-start.13
  16.6 0.0 collective-permute-start.7
  16.6 0.0 collective-permute-done.10
  16.6 0.5 %collective-permute-start.8 = (bf16[128,256]{1,0:T(8,128)(2,1)S(1)}, bf16[128,256]{1,0:T(8,128)(2,1)S(1)}, u32[]{:S(2)}, u32[]{:S(2)}) collective-permute-start(bf16[128,256]{1,0:T(8,128)(2,1)S(1)} %get-tuple-element.56), channel_id=1, source_target_pairs={{0,1},{1,0},{2,3},{3,2},{4,5},{5,4},{6,7},{7,6},{8,9},{9,8},{10,11... | collective-permute-start | bytes 196616 | tf_op jit(solution)/shard_map/ppermute | solution.py:163
  17.2 0.0 collective-permute-done.11
  17.2 0.2 collective-permute-done.3.near
  17.4 0.1 collective-permute-start.4
  17.5 0.5 %collective-permute-start.5 = (bf16[192,256]{1,0:T(8,128)(2,1)S(1)}, bf16[192,256]{1,0:T(8,128)(2,1)S(1)}, u32[]{:S(2)}, u32[]{:S(2)}) collective-permute-start(bf16[192,256]{1,0:T(8,128)(2,1)S(1)} %get-tuple-element.52), channel_id=1, source_target_pairs={{0,1},{1,0},{2,3},{3,2},{4,5},{5,4},{6,7},{7,6},{8,9},{9,8},{10,11... | collective-permute-start | bytes 294920 | tf_op jit(solution)/shard_map/ppermute | solution.py:163
  18.0 0.0 collective-permute-done.7
  18.0 0.1 collective-permute-done.8
  18.1 0.6 %shard_map.57 = (bf16[1,2,64,256]{3,2,1,0:T(8,128)(2,1)S(1)}, f32[1,2,64,256]{3,2,1,0:T(8,128)S(1)}) custom-call(s32[4,8,128]{2,1,0:T(8,128)S(1)} %get-tuple-element.33.used_ref, bf16[4,512,256]{2,1,0:T(8,128)(2,1)S(1)} %bitcast.31, bf16[2,128,256]{2,1,0:T(8,128)(2,1)S(1)} %collective-permute-done.1.psi, bf16[2,128,256]{2,1,0:T(8,128)(2,1)S(1)} %bitcast.41, ...), custom_call_target="tpu_custom_call" | custom-call | flops 2300000000 | tf_op jit(solution)/shard_map/pallas_call | solution.py:107
  18.7 2.0 %collective-permute-start.12 = (bf16[1,2,64,256]{3,2,1,0:T(8,128)(2,1)S(1)}, bf16[1,2,64,256]{3,2,1,0:T(8,128)(2,1)S(1)}, u32[]{:S(2)}, u32[]{:S(2)}) collective-permute-start(bf16[1,2,64,256]{3,2,1,0:T(8,128)(2,1)S(1)} %get-tuple-element.41), channel_id=1, source_target_pairs={{0,2},{2,0},{1,3},{3,1},{4,6},{6,4},{5,7},{7,5},{8,10},{10,8},{9,1... | collective-permute-start | bytes 196616 | tf_op jit(solution)/shard_map/ppermute | solution.py:200
  20.7 0.0 collective-permute-done.4
  20.7 0.0 collective-permute-done.5
  20.7 0.8 %collective-permute-done.13.psi = bf16[2,128,256]{2,1,0:T(8,128)(2,1)S(1)} collective-permute-done((bf16[2,128,256]{2,1,0:T(8,128)(2,1)S(1)}, bf16[2,128,256]{2,1,0:T(8,128)(2,1)S(1)}, u32[]{:S(2)}, u32[]{:S(2)}) %collective-permute-start.13) | collective-permute-done | bytes 131104 | tf_op jit(solution)/shard_map/ppermute | solution.py:160
  21.5 0.0 collective-permute-start.14
  21.5 0.6 %shard_map.56 = (bf16[1,2,64,256]{3,2,1,0:T(8,128)(2,1)S(1)}, f32[1,2,64,256]{3,2,1,0:T(8,128)S(1)}) custom-call(s32[4,8,128]{2,1,0:T(8,128)S(1)} %get-tuple-element.33.used_ref, bf16[4,512,256]{2,1,0:T(8,128)(2,1)S(1)} %bitcast.32, bf16[3,128,256]{2,1,0:T(8,128)(2,1)S(1)} %collective-permute-done.3.near, bf16[3,128,256]{2,1,0:T(8,128)(2,1)S(1)} %bitcast.40), custom_call_target="tpu_custom_call" | custom-call | flops 5750000128 | tf_op jit(solution)/shard_map/pallas_call | solution.py:107
  22.1 0.7 %collective-permute-start.6 = (bf16[1,2,64,256]{3,2,1,0:T(8,128)(2,1)S(1)}, bf16[1,2,64,256]{3,2,1,0:T(8,128)(2,1)S(1)}, u32[]{:S(2)}, u32[]{:S(2)}) collective-permute-start(bf16[1,2,64,256]{3,2,1,0:T(8,128)(2,1)S(1)} %get-tuple-element.38), channel_id=1, source_target_pairs={{0,2},{2,0},{1,3},{3,1},{4,6},{6,4},{5,7},{7,5},{8,10},{10,8},{9,1... | collective-permute-start | bytes 196616 | tf_op jit(solution)/shard_map/ppermute | solution.py:160
  22.8 0.0 collective-permute-done.14.other
  22.8 0.6 %shard_map.58 = (bf16[1,2,64,256]{3,2,1,0:T(8,128)(2,1)S(1)}, f32[1,2,64,256]{3,2,1,0:T(8,128)S(1)}) custom-call(s32[4,8,128]{2,1,0:T(8,128)S(1)} %get-tuple-element.33.used_ref, bf16[4,512,256]{2,1,0:T(8,128)(2,1)S(1)} %bitcast.33, bf16[2,128,256]{2,1,0:T(8,128)(2,1)S(1)} %collective-permute-done.13.psi, ...), custom_call_target="tpu_custom_call" | custom-call | tf_op jit(solution)/shard_map/pallas_call | solution.py:107
  23.5 1.4 %collective-permute-start.15 = (bf16[1,2,64,256]{3,2,1,0:T(8,128)(2,1)S(1)}, bf16[1,2,64,256]{3,2,1,0:T(8,128)(2,1)S(1)}, u32[]{:S(2)}, u32[]{:S(2)}) collective-permute-start(bf16[1,2,64,256]{3,2,1,0:T(8,128)(2,1)S(1)} %get-tuple-element.44), channel_id=1, source_target_pairs={{0,2},{2,0},{1,3},{3,1},{4,6},{6,4},{5,7},{7,5},{8,10},{10,8},{9,1... | collective-permute-start | bytes 196616 | tf_op jit(solution)/shard_map/ppermute | solution.py:204
  24.9 0.0 collective-permute-done.12.got_b
  24.9 2.1 %collective-permute-done.6.got_n = bf16[1,2,64,256]{3,2,1,0:T(8,128)(2,1)S(1)} collective-permute-done((bf16[1,2,64,256]{3,2,1,0:T(8,128)(2,1)S(1)}, bf16[1,2,64,256]{3,2,1,0:T(8,128)(2,1)S(1)}, u32[]{:S(2)}, u32[]{:S(2)}) %collective-permute-start.6) | collective-permute-done | bytes 65568 | tf_op jit(solution)/shard_map/ppermute | solution.py:160
  27.0 1.0 %collective-permute-done.15.got_c = bf16[1,2,64,256]{3,2,1,0:T(8,128)(2,1)S(1)} collective-permute-done((bf16[1,2,64,256]{3,2,1,0:T(8,128)(2,1)S(1)}, bf16[1,2,64,256]{3,2,1,0:T(8,128)(2,1)S(1)}, u32[]{:S(2)}, u32[]{:S(2)}) %collective-permute-start.15) | collective-permute-done | bytes 65568 | tf_op jit(solution)/shard_map/ppermute | solution.py:204
  28.1 0.8 %shard_map.59 = bf16[2,4,1,64,256]{4,3,2,1,0:T(8,128)(2,1)} custom-call(s32[4,8,128]{2,1,0:T(8,128)S(1)} %get-tuple-element.27.shown_ref, f32[1,2,64,256]{3,2,1,0:T(8,128)S(1)} %get-tuple-element.28.keep_m, bf16[1,2,64,256]{3,2,1,0:T(8,128)(2,1)S(1)} %collective-permute-done.2.got_m, f32[1,2,64,256]{3,2,1,0:T(8,128)S(1)} %get-tuple-element.37.keep_n, ...), custom_call_target="tpu_custom_call" | custom-call | tf_op jit(solution)/shard_map/pallas_call | solution.py:139
  (12 shorter events, 0.1 us)
Async XLA Ops:
  0.0 7.7 %copy-start = (bf16[4,1,512,256]{3,2,1,0:T(8,128)(2,1)S(1)}, bf16[4,1,512,256]{3,2,1,0:T(8,128)(2,1)}, u32[]{:S(2)}) copy-start(bf16[4,1,512,256]{3,2,1,0:T(8,128)(2,1)} %param.7) | copy-start | bytes 3145732
  0.0 14.3 %collective-permute-start.9 = (bf16[4,128,128]{2,1,0:T(8,128)(2,1)}, bf16[4,128,128]{2,1,0:T(8,128)(2,1)S(1)}, u32[]{:S(2)}, u32[]{:S(2)}) collective-permute-start(bf16[4,128,128]{2,1,0:T(8,128)(2,1)} %bitcast.36), channel_id=1, source_target_pairs={{0,8},{1,13},{4,12},{5,9},{8,0},{9,5},{12,4},{13,1},{2,10},{3,15},... | collective-permute-start | bytes 393224 | tf_op jit(solution)/shard_map/ppermute | solution.py:186
  5.1 0.9 %copy-start.1 = (bf16[4,1,128,128]{3,2,1,0:T(8,128)(2,1)S(1)}, bf16[4,1,128,128]{3,2,1,0:T(8,128)(2,1)}, u32[]{:S(2)}) copy-start(bf16[4,1,128,128]{3,2,1,0:T(8,128)(2,1)} %param.6) | copy-start | bytes 393220
  5.1 2.6 %collective-permute-start = (bf16[2,128,256]{2,1,0:T(8,128)(2,1)S(1)}, bf16[2,128,256]{2,1,0:T(8,128)(2,1)S(1)}, u32[]{:S(2)}, u32[]{:S(2)}) collective-permute-start(bf16[2,128,256]{2,1,0:T(8,128)(2,1)S(1)} %constant_dynamic-update-slice_fusion.mine), channel_id=1, source_target_pairs={{0,1},{1,0},{2,3},{3,2},{4,5},{5,4},{6,7},{7,6},{8,9},{9,8},{10,11... | collective-permute-start | bytes 393224 | tf_op jit(solution)/shard_map/ppermute | solution.py:160
  5.8 10.7 %collective-permute-start.1 = (bf16[2,128,256]{2,1,0:T(8,128)(2,1)S(1)}, bf16[2,128,256]{2,1,0:T(8,128)(2,1)S(1)}, u32[]{:S(2)}, u32[]{:S(2)}) collective-permute-start(bf16[2,128,256]{2,1,0:T(8,128)(2,1)S(1)} %pad_maximum_fusion.2), channel_id=1, source_target_pairs={{0,8},{2,14},{4,12},{6,10},{8,0},{10,6},{12,4},{14,2},{1,9},{3,15}... | collective-permute-start | bytes 393224 | tf_op jit(solution)/shard_map/ppermute | solution.py:187
  6.0 1.7 %copy-start.2 = (s32[4,4]{1,0:T(4,128)S(1)}, s32[4,4]{1,0:T(4,128)}, u32[]{:S(2)}) copy-start(s32[4,4]{1,0:T(4,128)} %live_hbm.1) | copy-start | bytes 196
  6.1 1.7 %copy-start.3 = (s32[4]{0:T(128)S(1)}, s32[4]{0:T(128)}, u32[]{:S(2)}) copy-start(s32[4]{0:T(128)} %rows_hbm.1) | copy-start | bytes 52
  6.1 11.3 %collective-permute-start.3 = (bf16[3,128,256]{2,1,0:T(8,128)(2,1)S(1)}, bf16[3,128,256]{2,1,0:T(8,128)(2,1)S(1)}, u32[]{:S(2)}, u32[]{:S(2)}) collective-permute-start(bf16[3,128,256]{2,1,0:T(8,128)(2,1)S(1)} %pad_maximum_fusion), channel_id=1, source_target_pairs={{0,4},{4,0},{8,12},{12,8},{1,5},{5,1},{9,13},{13,9},{2,6},{6,2},{1... | collective-permute-start | bytes 589832 | tf_op jit(solution)/shard_map/ppermute | solution.py:156
  8.6 7.8 %collective-permute-start.2 = (bf16[1,2,64,256]{3,2,1,0:T(8,128)(2,1)S(1)}, bf16[1,2,64,256]{3,2,1,0:T(8,128)(2,1)S(1)}, u32[]{:S(2)}, u32[]{:S(2)}) collective-permute-start(bf16[1,2,64,256]{3,2,1,0:T(8,128)(2,1)S(1)} %get-tuple-element.31), channel_id=1, source_target_pairs={{0,2},{2,0},{1,3},{3,1},{4,6},{6,4},{5,7},{7,5},{8,10},{10,8},{9,1... | collective-permute-start | bytes 196616 | tf_op jit(solution)/shard_map/ppermute | solution.py:160
  14.3 2.4 %collective-permute-start.10 = (bf16[256,128]{1,0:T(8,128)(2,1)S(1)}, bf16[256,128]{1,0:T(8,128)(2,1)S(1)}, u32[]{:S(2)}, u32[]{:S(2)}) collective-permute-start(bf16[256,128]{1,0:T(8,128)(2,1)S(1)} %bitcast.43), channel_id=1, source_target_pairs={{0,1},{1,0},{2,3},{3,2},{4,5},{5,4},{6,7},{7,6},{8,9},{9,8},{10,11... | collective-permute-start | bytes 196616 | tf_op jit(solution)/shard_map/ppermute | solution.py:163
  14.4 2.8 %collective-permute-start.11 = (bf16[256,128]{1,0:T(8,128)(2,1)S(1)}, bf16[256,128]{1,0:T(8,128)(2,1)S(1)}, u32[]{:S(2)}, u32[]{:S(2)}) collective-permute-start(bf16[256,128]{1,0:T(8,128)(2,1)S(1)} %bitcast.42), channel_id=1, source_target_pairs={{0,1},{1,0},{2,3},{3,2},{4,5},{5,4},{6,7},{7,6},{8,9},{9,8},{10,11... | collective-permute-start | bytes 196616 | tf_op jit(solution)/shard_map/ppermute | solution.py:163
  16.5 5.0 %collective-permute-start.13 = (bf16[2,128,256]{2,1,0:T(8,128)(2,1)S(1)}, bf16[2,128,256]{2,1,0:T(8,128)(2,1)S(1)}, u32[]{:S(2)}, u32[]{:S(2)}) collective-permute-start(bf16[2,128,256]{2,1,0:T(8,128)(2,1)S(1)} %collective-permute-done.1.psi), channel_id=1, source_target_pairs={{0,2},{2,0},{1,3},{3,1},{4,6},{6,4},{5,7},{7,5},{8,10},{10,8},{9,1... | collective-permute-start | bytes 393224 | tf_op jit(solution)/shard_map/ppermute | solution.py:160
  16.6 1.3 %collective-permute-start.7 = (bf16[128,256]{1,0:T(8,128)(2,1)S(1)}, bf16[128,256]{1,0:T(8,128)(2,1)S(1)}, u32[]{:S(2)}, u32[]{:S(2)}) collective-permute-start(bf16[128,256]{1,0:T(8,128)(2,1)S(1)} %get-tuple-element.55), channel_id=1, source_target_pairs={{0,1},{1,0},{2,3},{3,2},{4,5},{5,4},{6,7},{7,6},{8,9},{9,8},{10,11... | collective-permute-start | bytes 196616 | tf_op jit(solution)/shard_map/ppermute | solution.py:163
  16.6 1.4 %collective-permute-start.8 = (bf16[128,256]{1,0:T(8,128)(2,1)S(1)}, bf16[128,256]{1,0:T(8,128)(2,1)S(1)}, u32[]{:S(2)}, u32[]{:S(2)}) collective-permute-start(bf16[128,256]{1,0:T(8,128)(2,1)S(1)} %get-tuple-element.56), channel_id=1, source_target_pairs={{0,1},{1,0},{2,3},{3,2},{4,5},{5,4},{6,7},{7,6},{8,9},{9,8},{10,11... | collective-permute-start | bytes 196616 | tf_op jit(solution)/shard_map/ppermute | solution.py:163
  17.4 3.3 %collective-permute-start.4 = (bf16[192,256]{1,0:T(8,128)(2,1)S(1)}, bf16[192,256]{1,0:T(8,128)(2,1)S(1)}, u32[]{:S(2)}, u32[]{:S(2)}) collective-permute-start(bf16[192,256]{1,0:T(8,128)(2,1)S(1)} %get-tuple-element.51), channel_id=1, source_target_pairs={{0,1},{1,0},{2,3},{3,2},{4,5},{5,4},{6,7},{7,6},{8,9},{9,8},{10,11... | collective-permute-start | bytes 294920 | tf_op jit(solution)/shard_map/ppermute | solution.py:163
  17.5 3.2 %collective-permute-start.5 = (bf16[192,256]{1,0:T(8,128)(2,1)S(1)}, bf16[192,256]{1,0:T(8,128)(2,1)S(1)}, u32[]{:S(2)}, u32[]{:S(2)}) collective-permute-start(bf16[192,256]{1,0:T(8,128)(2,1)S(1)} %get-tuple-element.52), channel_id=1, source_target_pairs={{0,1},{1,0},{2,3},{3,2},{4,5},{5,4},{6,7},{7,6},{8,9},{9,8},{10,11... | collective-permute-start | bytes 294920 | tf_op jit(solution)/shard_map/ppermute | solution.py:163
  18.7 6.2 %collective-permute-start.12 = (bf16[1,2,64,256]{3,2,1,0:T(8,128)(2,1)S(1)}, bf16[1,2,64,256]{3,2,1,0:T(8,128)(2,1)S(1)}, u32[]{:S(2)}, u32[]{:S(2)}) collective-permute-start(bf16[1,2,64,256]{3,2,1,0:T(8,128)(2,1)S(1)} %get-tuple-element.41), channel_id=1, source_target_pairs={{0,2},{2,0},{1,3},{3,1},{4,6},{6,4},{5,7},{7,5},{8,10},{10,8},{9,1... | collective-permute-start | bytes 196616 | tf_op jit(solution)/shard_map/ppermute | solution.py:200
  21.5 1.3 %collective-permute-start.14 = (bf16[2,128,256]{2,1,0:T(8,128)(2,1)S(1)}, bf16[2,128,256]{2,1,0:T(8,128)(2,1)S(1)}, u32[]{:S(2)}, u32[]{:S(2)}) collective-permute-start(bf16[2,128,256]{2,1,0:T(8,128)(2,1)S(1)} %collective-permute-done.13.psi), channel_id=1, source_target_pairs={{0,1},{1,0},{2,3},{3,2},{4,5},{5,4},{6,7},{7,6},{8,9},{9,8},{10,11... | collective-permute-start | bytes 393224 | tf_op jit(solution)/shard_map/ppermute | solution.py:160
  22.1 4.9 %collective-permute-start.6 = (bf16[1,2,64,256]{3,2,1,0:T(8,128)(2,1)S(1)}, bf16[1,2,64,256]{3,2,1,0:T(8,128)(2,1)S(1)}, u32[]{:S(2)}, u32[]{:S(2)}) collective-permute-start(bf16[1,2,64,256]{3,2,1,0:T(8,128)(2,1)S(1)} %get-tuple-element.38), channel_id=1, source_target_pairs={{0,2},{2,0},{1,3},{3,1},{4,6},{6,4},{5,7},{7,5},{8,10},{10,8},{9,1... | collective-permute-start | bytes 196616 | tf_op jit(solution)/shard_map/ppermute | solution.py:160
  23.5 4.6 %collective-permute-start.15 = (bf16[1,2,64,256]{3,2,1,0:T(8,128)(2,1)S(1)}, bf16[1,2,64,256]{3,2,1,0:T(8,128)(2,1)S(1)}, u32[]{:S(2)}, u32[]{:S(2)}) collective-permute-start(bf16[1,2,64,256]{3,2,1,0:T(8,128)(2,1)S(1)} %get-tuple-element.44), channel_id=1, source_target_pairs={{0,2},{2,0},{1,3},{3,1},{4,6},{6,4},{5,7},{7,5},{8,10},{10,8},{9,1... | collective-permute-start | bytes 196616 | tf_op jit(solution)/shard_map/ppermute | solution.py:204
